TPU v7x, 32 devices: a whole 2x2x4 slice. The times are simulated.
32 devices in a mesh: ctx: 8 (over z, y), head: 4 (over x, core).
Axes of the slice: x: 2, y: 2, z: 4, core: 2. Of those that a mesh axis runs over, the one named last changes fastest.
Arguments:
- queries: bfloat16 [8192, 12288], P('ctx', 'head'), may hold values from -24 to 24
- key_rows: bfloat16 [8192, 768], P('ctx'), may hold values from -6 to 6
- value_rows: bfloat16 [8192, 512], P('ctx'), may hold values from -6 to 6
- comp_key_weight: float32 [32, 768], replicated, may hold values from 0.35355338 to 0.70710677
- comp_value_weight: float32 [32, 512], replicated, may hold values from 0.17677669 to 0.53033006
- block_picks: int32 [32, 4, 16], P('ctx'), may hold values from 0 to 124, as said below
- gate_logits: float32 [8192, 3, 64], P('ctx', None, 'head'), may hold values from -6 to 6
- out_weight: bfloat16 [8192, 2560], P('head'), may hold values from -0.25 to 0.25
Outputs:
- layer_out: bfloat16 [8192, 2560], P(('ctx', 'head'))
Inputs may be any that keep to these rules, and one draw needn't show every extreme that they name: `block_picks`: for each group, the lists of the 256-position query blocks held by one ctx shard name exactly 1024 / 256 distinct blocks of each earlier shard and of their own shard, and none of later shards; the own-shard blocks named are the first blocks of those query blocks. Every list names the first block of its own query block. Names may repeat within a list.
All inputs are finite; a program needn't handle non-finite values.
Results may differ from a plain program's by a relative error of at most 0.03.
Values may be sent and summed in bfloat16 or wider, within the bound.
No kernel may reach another device: no remote copies, remote signals or barrier semaphores. Data moves between devices by JAX's collectives and lax.ppermute only.
A program may use at most 192 MiB of HBM per device.

v0:
```python
import functools

import jax
import jax.numpy as jnp
from jax import lax
from jax.experimental import pallas as pl
from jax.experimental.pallas import tpu as pltpu
from jax.sharding import PartitionSpec as P

HEADS = 64
GROUPS = 4
QK = 192
DV = 128
CBLK = 32
KBLK = 64
PICKS = 16
WINDOW = 512
QBLK = 256
PAIR = 2 * QK
BROWS = KBLK + KBLK // 2 + KBLK
VMEM_LIMIT = 50 * 1024 * 1024
CHOSEN_LIMIT = 48 * 1024 * 1024
NEG = -1e30
SCALE = QK ** (-0.5) * 1.4426950408889634
LOW_TOTAL, HIGH_TOTAL = 2.0**-60, 2.0**100
TILE = 256
NT = (((1,), (1,)), ((), ()))
F32 = jnp.float32
BF16 = jnp.bfloat16


def half_lanes(rows):
    return lax.broadcasted_iota(jnp.int32, (rows, 128), 1) < 64


def swap_halves(x):
    return pltpu.roll(x, 64, 1)


def turned(keys):
    row, col = iota(256, 256, 0), iota(256, 256, 1)
    unit = (row == col).astype(BF16)
    even = lax.dot_general(unit, keys, NT, preferred_element_type=F32).astype(BF16)
    return even, lower(even)


def lower(even):
    return jnp.concatenate([jnp.zeros((64, even.shape[1]), BF16), even[:QK]], axis=0)


def with_ones(values):
    return jnp.concatenate([values, jnp.ones_like(values)], axis=1)


def plan(group, shard, per_owner, picks_ref, lists_ref, slots_ref, dead_ref):
    lists = picks_ref.shape[0]
    total = lists_ref.shape[1] // lists * per_owner
    width = slots_ref.shape[1]
    picks = jnp.zeros((lists, PICKS), jnp.int32)
    for each in range(picks_ref.shape[1]):
        picks = jnp.where(group == each, picks_ref[:, each, :], picks)
    block = iota(lists, total, 1)
    hits = [block == picks[:, entry : entry + 1] for entry in range(PICKS)]
    named = functools.reduce(jnp.logical_or, hits).astype(F32)
    named = jnp.broadcast_to(jnp.max(named, axis=0, keepdims=True), (8, total))
    row, col = iota(total, total, 0), iota(total, total, 1)
    before = (lax.div(row, per_owner) == lax.div(col, per_owner)) & (row < col)
    rank = jnp.dot(named, before.astype(F32), preferred_element_type=F32)
    rank = jnp.minimum(rank, float(lists - 1))
    inside = lax.rem(iota(8, total, 1), per_owner).astype(F32)
    found = jnp.zeros((8, lists_ref.shape[1]), F32)
    row, col = iota(total, lists_ref.shape[1], 0), iota(total, lists_ref.shape[1], 1)
    for place in range(lists):
        to = (col == lax.div(row, per_owner) * lists + place).astype(F32)
        value = jnp.where(rank == float(place), named * inside, 0.0)
        found = found + jnp.dot(value, to, preferred_element_type=F32)
    lists_ref[...] = found[:1].astype(jnp.int32)

    owner = lax.div(block, per_owner)
    turn = (lax.div(shard, 2) - lax.div(owner, 2)) * 2 + ((owner ^ shard) & 1)
    slot = jnp.clip(turn * lists + rank[:lists].astype(jnp.int32), 0, lists_ref.shape[1] - 1)
    slot = slot.astype(F32)
    first = shard * per_owner + iota(lists, 1, 0) * (QBLK // KBLK)
    own = block == first

    def pick_out(hit, values):
        return jnp.sum(jnp.where(hit, values, 0.0), axis=1, keepdims=True)

    lane = iota(lists, width, 1)
    slots = jnp.where(lane == 0, pick_out(own, slot), 0.0)
    dead = jnp.zeros((lists, width), F32)
    seen = own.astype(F32)
    at = jnp.ones((lists, 1), jnp.int32)
    met = jnp.zeros((lists, 1), jnp.int32)
    for entry, hit in enumerate(hits):
        pick = picks[:, entry : entry + 1]
        is_own = (pick == first).astype(jnp.int32)
        gone = jnp.maximum(pick_out(hit, seen), (pick > first).astype(F32))
        slots = jnp.where(lane == at, pick_out(hit, slot), slots)
        dead = jnp.where(lane == at, gone, dead)
        seen = jnp.maximum(seen, hit.astype(F32))
        at = at + 1 - is_own * (1 - met)
        met = jnp.maximum(met, is_own)
    slots_ref[...] = slots.astype(jnp.int32)
    dead_ref[...] = dead.astype(jnp.int32)


def prep_kernel(
    where_ref,
    picks_in,
    keys_in,
    values_in,
    fold_in,
    packed_ref,
    rim_ref,
    lists_ref,
    slots_ref,
    dead_ref,
    even_ref,
    odd_ref,
    val_ref,
    picks_ref,
    keys_ref,
    values_ref,
    kw_ref,
    vw_ref,
    sems,
):
    group, shard = where_ref[0], where_ref[1]
    pair = pl.ds(pl.multiple_of(lax.div(group, 2) * PAIR, 128), PAIR)
    single = pl.ds(pl.multiple_of(group * DV, 128), DV)
    folded_value = pl.ds(pl.multiple_of(GROUPS * QK + group * DV, 128), DV)
    copies = [
        pltpu.make_async_copy(source, target, sems.at[i])
        for i, (source, target) in enumerate(
            [
                (picks_in, picks_ref),
                (keys_in.at[:, pair], keys_ref),
                (values_in.at[:, single], values_ref),
                (fold_in.at[:, pair], kw_ref),
                (fold_in.at[:, folded_value], vw_ref),
            ]
        )
    ]
    for copy in copies:
        copy.start()
    copies[0].wait()
    plan(group, shard, keys_ref.shape[0] // KBLK, picks_ref, lists_ref, slots_ref, dead_ref)
    for copy in copies[1:]:
        copy.wait()
    odd = lax.rem(group, 2) == 1

    def own_columns(ref):
        t0 = ref[:, :128].astype(F32)
        t1 = ref[:, 128:256].astype(F32)
        t2 = ref[:, 256:].astype(F32)
        r1, r2 = swap_halves(t1), swap_halves(t2)
        left = half_lanes(t0.shape[0])
        low = jnp.where(odd, jnp.where(left, r1, r2), t0)
        high = jnp.where(left, jnp.where(odd, r2, t1), 0.0)
        return low, high

    low, high = own_columns(keys_ref)
    values = values_ref[...]
    rows = low.shape[0]
    count = rows // KBLK
    high3 = high.reshape(count, KBLK, 128)
    packed_high = high3[:, : KBLK // 2] + swap_halves(
        high3[:, KBLK // 2 :].reshape(count * KBLK // 2, 128)
    ).reshape(count, KBLK // 2, 128)
    even = jnp.concatenate([low.astype(BF16), high.astype(BF16)], axis=1)
    even_ref[...], odd_ref[...] = turned(even)
    val_ref[...] = with_ones(values)
    for block in range(count):
        at = block * BROWS
        token = slice(block * KBLK, block * KBLK + KBLK)
        packed_ref[at : at + KBLK] = low[token].astype(BF16)
        packed_ref[at + KBLK : at + KBLK + KBLK // 2] = packed_high[block].astype(BF16)
        packed_ref[at + KBLK + KBLK // 2 : at + BROWS] = values[token]
    rim_rows = rim_ref.shape[0]
    rim_ref[...] = packed_ref[count * BROWS - rim_rows : count * BROWS]

    wlow, whigh = own_columns(kw_ref)
    folds = rows // CBLK

    def fold(x, w):
        return jnp.sum(x.reshape(folds, CBLK, 128) * w[None], axis=1).astype(BF16)

    at = count * BROWS
    packed_ref[at : at + folds] = fold(low, wlow)
    packed_ref[at + folds : at + 2 * folds] = fold(high, whigh)
    packed_ref[at + 2 * folds :] = fold(values.astype(F32), vw_ref[...])


def pack_kernel(lists, beside, where_ref, *refs):
    count = len(refs) // 2
    named, ref, outs = refs[:count], refs[count], refs[count + 1 :]
    shard = where_ref[1]
    owner = shard + 1 - 2 * lax.rem(shard, 2) if beside else shard
    data = ref.shape[0] - (outs[0].shape[0] - lists * BROWS)
    for blocks, out in zip(named, outs):
        for place in range(lists):
            at = pl.multiple_of(blocks[0, owner * lists + place] * BROWS, 16)
            out[place * BROWS : (place + 1) * BROWS] = ref[pl.ds(at, BROWS)]
        out[lists * BROWS :] = ref[data:]


def unpack(ref, at, count, step=1):
    lows, packed, values = [], [], []
    for block in range(count):
        first = at + block * step * BROWS
        lows.append(ref[first : first + KBLK])
        packed.append(ref[first + KBLK : first + KBLK + KBLK // 2])
        values.append(ref[first + KBLK + KBLK // 2 : first + BROWS])
    packed = jnp.concatenate(packed, axis=0)
    row, col = iota(128, 256, 0), iota(128, 256, 1)
    take = (row == jnp.where(col < 128, col, col - 64)) & (lax.rem(col, 128) < 64)
    both = jnp.dot(packed, take.astype(BF16), preferred_element_type=F32).astype(BF16)
    half = KBLK // 2
    highs = []
    for block in range(count):
        rows = slice(block * half, block * half + half)
        highs += [both[rows, :128], both[rows, 128:]]
    even = jnp.concatenate(
        [jnp.concatenate(lows, axis=0), jnp.concatenate(highs, axis=0)], axis=1
    )
    return even, jnp.concatenate(values, axis=0)


def fill_rim(shard, near_ref, far_ref, own, ext):
    rim_blocks = WINDOW // KBLK
    even_in, odd_in, val_in = own
    even_ref, odd_ref, val_ref = ext
    even_ref[:, WINDOW:] = even_in[:, :WINDOW]
    odd_ref[:, WINDOW:] = odd_in[:, :WINDOW]
    val_ref[WINDOW:] = val_in[:WINDOW]
    use_near = lax.rem(shard, 2) == 1
    rim_end = near_ref.shape[0] // BROWS * BROWS
    near_rim = near_ref[rim_end - far_ref.shape[0] : rim_end]

    @pl.when(shard > 0)
    def _():
        keys, values = unpack(jnp.where(use_near, near_rim, far_ref[...]), 0, rim_blocks)
        even_ref[:, :WINDOW], odd_ref[:, :WINDOW] = turned(keys)
        val_ref[:WINDOW] = with_ones(values)

    @pl.when(shard == 0)
    def _():
        even = jnp.broadcast_to(even_in[:, :1].astype(F32), (256, WINDOW)).astype(BF16)
        even_ref[:, :WINDOW], odd_ref[:, :WINDOW] = even, lower(even)
        val_ref[:WINDOW] = jnp.zeros((WINDOW, 256), BF16)


def pool_kernel(groups, lists, where_ref, own_ref, *refs):
    sent = 2 * groups - 1
    ins, (key_ref, val_ref, ceven_ref, codd_ref, cval_ref, folded) = refs[:sent], refs[sent:]
    shard = where_ref[1]
    parity = lax.rem(shard, 2)
    base = shard - parity
    rows = lists * KBLK
    folds = (ins[0].shape[0] - lists * BROWS) // 3
    folded[...] = jnp.zeros_like(folded)
    cval_ref[...] = jnp.zeros_like(cval_ref)

    def fill(place, owner, ref, step, fold_at):
        keys, values = unpack(ref, 0, lists, step)
        at = slice(place * rows, place * rows + rows)
        key_ref[at] = keys
        val_ref[at] = values
        low = ref[fold_at : fold_at + folds]
        high = ref[fold_at + folds : fold_at + 2 * folds]
        owned = pl.ds(pl.multiple_of(owner * folds, 32), folds)
        folded[owned] = jnp.concatenate([low, high], axis=1)
        cval_ref[owned] = with_ones(ref[fold_at + 2 * folds : fold_at + 3 * folds])

    fill(0, shard, own_ref, QBLK // KBLK, own_ref.shape[0] - 3 * folds)
    fill(1, base + 1 - parity, ins[0], 1, lists * BROWS)
    for distance in range(1, groups):

        @pl.when(base >= 2 * distance)
        def _():
            for side in range(2):
                owner = base - 2 * distance + (parity if side == 0 else 1 - parity)
                fill(2 * distance + side, owner, ins[2 * (groups - distance) - 1 + side], 1, lists * BROWS)

    ceven_ref[...], codd_ref[...] = turned(folded[...])


def iota(rows, cols, axis):
    return lax.broadcasted_iota(jnp.int32, (rows, cols), axis)


def scores_of(q, keys, mask):
    scores = jnp.dot(q, keys, preferred_element_type=F32)
    return scores if mask is None else mask(scores)


def in_range(total):
    good = jnp.where((total >= LOW_TOTAL) & (total <= HIGH_TOTAL), 1.0, 0.0)
    return jnp.min(good.reshape(-1, 8, DV), axis=0)


def over_heads(pairs, load, branches, finish):
    def sums(weights, values):
        out = jnp.dot(weights, values(), preferred_element_type=F32)
        return out[:, :DV], out[:, DV:]

    at_once = 2 if pairs % 2 == 0 else 1
    units = [(pair, side) for pair in range(0, pairs, at_once) for side in range(2)]
    worst, held = [], None
    for now, unit in zip([None] + units, units + [None]):
        q = None if unit is None else load(*unit, at_once)
        fresh, parts = [], []
        for at, (tiles, values) in enumerate(branches):
            weights, ahead = [], []
            for place, (keys, mask) in enumerate(tiles):
                if q is not None:
                    ahead.append(scores_of(q, keys(unit[1]), mask))
                if held is not None:
                    weights.append(jnp.exp2(held[at][place] * SCALE).astype(BF16))
            fresh.append(ahead)
            parts.append((weights, values))
        if held is not None:
            parts = [sums(jnp.concatenate(w, axis=1), values) for w, values in parts]
            worst += [in_range(x) for x in finish(*now, at_once, parts)]
        held = fresh

    @pl.when(jnp.min(functools.reduce(jnp.minimum, worst)) < 0.5)
    def _():
        def exact(pair, _):
            for side in range(2):
                q = load(pair, side, 1)
                parts = []
                for tiles, values in branches:
                    scores = [scores_of(q, keys(side), mask) for keys, mask in tiles]
                    scores = jnp.concatenate(scores, axis=1)
                    top = jnp.max(scores, axis=1, keepdims=True)
                    shifted = (scores - jnp.maximum(top, -1e28)) * SCALE
                    parts.append(sums(jnp.exp2(shifted).astype(BF16), values))
                finish(pair, side, 1, parts)
            return 0

        lax.fori_loop(0, pairs, exact, 0)


def aligned(at):
    return at if isinstance(at, int) else pl.multiple_of(at, 128)


def query_loader(q_ref):
    def load(pair, side, n):
        at = [aligned((pair + p) * PAIR + side * 128) for p in range(n)]
        return jnp.concatenate([q_ref[:, pl.ds(x, 256)] for x in at], axis=0)

    return load


def head_columns(pair, side):
    return pl.ds(aligned(pair * 2 * DV + side * DV), DV)


def gate_loader(gate_ref, first, heads):
    turned = pltpu.roll(gate_ref[...], lax.rem(128 - first, 128), 1)

    def load(pair, side, n, branch):
        if isinstance(pair, int):
            local, at = turned, branch * heads + side + 2 * pair
        else:
            local, at = pltpu.roll(turned, lax.rem(128 - 2 * pair, 128), 1), branch * heads + side
        columns = [local[:, at + 2 * p : at + 2 * p + 1] for p in range(n)]
        shape = (turned.shape[0], DV)
        return jnp.concatenate([jnp.broadcast_to(x, shape) for x in columns], axis=0)

    return load


def stacked(x, times):
    return jnp.concatenate([x] * times, axis=0) if times > 1 else x


def repeated(keep, rows):
    return stacked(keep, rows // keep.shape[0])


def near_kernel(heads, first_block, rim, where_ref, q_ref, gate_ref, *refs):
    keys = refs[:3]
    if rim:
        out_ref, ext = refs[-4], refs[-3:]

        @pl.when((pl.program_id(0) == 0) & (pl.program_id(1) == 0))
        def _():
            fill_rim(where_ref[1], refs[3], refs[4], keys, ext)

        keys, reach = ext, 0
    else:
        out_ref, reach = refs[-1], WINDOW
    count = q_ref.shape[1] // QK
    gate = gate_loader(gate_ref, pl.program_id(1) * count, heads)
    base = pl.multiple_of((first_block + pl.program_id(0)) * QBLK - reach, QBLK)
    row, col = iota(QBLK, QBLK, 0), iota(QBLK, QBLK, 1)

    def tile(place, mask):
        return (lambda side: keys[side][:, pl.ds(base + place * QBLK, QBLK)]), mask

    def finish(pair, side, n, parts):
        ((num, den),) = parts
        total = gate(pair, side, n, 2) * (num / den)
        for p in range(n):
            part = total[p * QBLK : (p + 1) * QBLK]
            out_ref[:, head_columns(pair + p, side)] = part.astype(BF16)
        return [den]

    tiles = [
        tile(0, lambda x: jnp.where(repeated(col >= row, x.shape[0]), x, NEG)),
        tile(1, None),
        tile(2, lambda x: jnp.where(repeated(col <= row, x.shape[0]), x, NEG)),
    ]
    values = lambda: keys[2][pl.ds(base, WINDOW + QBLK)]
    over_heads(count // 2, query_loader(q_ref), [(tiles, values)], finish)


def near_branch(first_block, block_count, where, queries, gates, keys, rims, prior):
    tokens, width = queries.shape
    heads = width // QK
    at_once = next(n for n in (8, 4, 2) if heads % n == 0)
    row_block = lambda i, p, *_: (i + first_block, p)
    operands = [queries, gates, *keys]
    specs = [
        pl.BlockSpec((QBLK, at_once * QK), row_block),
        pl.BlockSpec((QBLK, 128), lambda i, p, *_: (i + first_block, 0)),
    ]
    specs += [VMEM_SPEC] * len(keys)
    alias, scratch = {}, []
    if rims is not None:
        other, far = rims
        operands += [other, far]
        specs += [VMEM_SPEC, VMEM_SPEC]
        scratch = [pltpu.VMEM((256, 2 * WINDOW), BF16)] * 2 + [pltpu.VMEM((2 * WINDOW, 256), BF16)]
    if prior is not None:
        operands.append(prior)
        specs.append(pl.BlockSpec(memory_space=pl.ANY))
        alias = {len(operands): 0}
    rows = block_count * QBLK * heads
    return pl.pallas_call(
        functools.partial(near_kernel, heads, first_block, rims is not None),
        grid_spec=pltpu.PrefetchScalarGridSpec(
            num_scalar_prefetch=1,
            grid=(block_count, heads // at_once),
            in_specs=specs,
            out_specs=pl.BlockSpec((QBLK, at_once * DV), row_block),
            scratch_shapes=scratch,
        ),
        out_shape=jax.ShapeDtypeStruct((tokens, heads * DV), BF16),
        input_output_aliases=alias,
        compiler_params=pltpu.CompilerParams(vmem_limit_bytes=VMEM_LIMIT),
        cost_estimate=pl.CostEstimate(
            flops=rows * (WINDOW + QBLK) * 64,
            bytes_accessed=rows * (2 * QK + 4 * DV),
            transcendentals=0,
        ),
        name="near_branch",
    )(where, *operands)


def chosen_kernel(heads, span, *refs):
    first_chunk, widths = span
    out_count = sum(len(w) for w in widths)
    meta_ref, slots_ref, dead_ref, q_ref, gate_ref, near_ref = refs[:6]
    (key_pool, val_pool), cfold, weight_ref = refs[6:8], refs[8:11], refs[11]
    outs = list(refs[12 : 12 + out_count])
    gathered, even, odd, val, attended, weight, weight_sem = refs[12 + out_count :]
    keys = (even, odd)
    turn, step = pl.program_id(0), pl.program_id(1)
    last = pl.num_programs(1) - 1
    rows = q_ref.shape[0]
    count = q_ref.shape[1] // QK
    chunk_start = meta_ref[2 + first_chunk + turn] * rows
    list_at = lax.div(chunk_start, QBLK)
    first_row = lax.rem(chunk_start, QBLK)
    position = meta_ref[2] + chunk_start
    copy = pltpu.make_async_copy(weight_ref, weight, weight_sem)

    @pl.when(step == 0)
    def _():
        for slot in range(PICKS):
            source = pl.multiple_of(slots_ref[list_at, slot] * KBLK, KBLK)
            gathered[slot * KBLK : (slot + 1) * KBLK] = key_pool[pl.ds(source, KBLK)]
            val[slot * KBLK : (slot + 1) * KBLK] = with_ones(val_pool[pl.ds(source, KBLK)])
        for slot in range(1, PICKS):

            @pl.when(dead_ref[list_at, slot] == 1)
            def _():
                at = slice(slot * KBLK, (slot + 1) * KBLK)
                gathered[at] = jnp.broadcast_to(gathered[:1], (KBLK, 256))
                val[at] = jnp.zeros((KBLK, 256), BF16)

        even[...], odd[...] = turned(gathered[...])

    @pl.when((turn == 0) & (step == 0))
    def _():
        copy.start()

    gate = gate_loader(gate_ref, step * count, heads)
    row = iota(rows, TILE, 0)
    col = iota(rows, TILE, 1)
    own_keep = (col >= KBLK) | (col <= row + first_row)

    def own_mask(scores):
        own = jnp.where(repeated(own_keep[:, :128], scores.shape[0]), scores[:, :128], NEG)
        return jnp.concatenate([own, scores[:, 128:]], axis=1)

    def comp_mask(place):
        ends = (col + place * TILE + 1) * CBLK - 1
        return lambda x: jnp.where(repeated(ends <= row + position, x.shape[0]), x, NEG)

    def tile(refs, place, mask):
        return (lambda side: refs[side][:, place * TILE : (place + 1) * TILE]), mask

    chosen = [tile(keys, p, own_mask if p == 0 else None) for p in range(PICKS * KBLK // TILE)]
    folded = [tile(cfold, p, comp_mask(p)) for p in range(cfold[2].shape[0] // TILE)]
    empty = row[:, :DV] + position < CBLK - 1

    def finish(pair, side, n, parts):
        (num, den), (folded_num, folded_den) = parts
        folded_den = jnp.where(stacked(empty, n), 1.0, folded_den)
        total = gate(pair, side, n, 1) * (num / den)
        total = total + gate(pair, side, n, 0) * (folded_num / folded_den)
        for p in range(n):
            cols = head_columns(pair + p, side)
            mixed = near_ref[:, cols].astype(F32) + total[p * rows : (p + 1) * rows]
            attended[step, :, cols] = mixed.astype(BF16)
        return [den, folded_den]

    branches = [(chosen, lambda: val[...]), (folded, lambda: cfold[2][...])]
    over_heads(count // 2, query_loader(q_ref), branches, finish)

    @pl.when((turn == 0) & (step == last))
    def _():
        copy.wait()

    for place, parts in enumerate(widths):
        chunk_outs = [outs.pop(0) for _ in parts]

        @pl.when((turn == place) & (step == last))
        def _():
            rows_in = jnp.concatenate([attended[s] for s in range(attended.shape[0])], axis=1)
            first_col = 0
            for out_ref in chunk_outs:
                for at in range(0, out_ref.shape[1], 256):
                    cols = weight[:, first_col + at : first_col + at + 256]
                    part = jnp.dot(rows_in, cols, preferred_element_type=F32)
                    out_ref[:, at : at + 256] = part.astype(out_ref.dtype)
                first_col += out_ref.shape[1]


def chosen_and_project(first_chunk, widths, rows, meta, slots, dead, queries, gates, near, pools, out_weight):
    tokens, width = queries.shape
    heads = width // QK
    at_once = next(n for n in (8, 4, 2) if heads % n == 0)
    steps = heads // at_once
    whole = lambda x: pl.BlockSpec(x.shape, lambda i, p, *_: (0,) * x.ndim)
    outs = [jax.ShapeDtypeStruct((rows, width), BF16) for chunk in widths for width in chunk]
    return pl.pallas_call(
        functools.partial(chosen_kernel, heads, (first_chunk, widths)),
        grid_spec=pltpu.PrefetchScalarGridSpec(
            num_scalar_prefetch=3,
            grid=(len(widths), steps),
            in_specs=[
                pl.BlockSpec((rows, at_once * QK), lambda i, p, m, *_: (m[2 + first_chunk + i], p)),
                pl.BlockSpec((rows, 128), lambda i, p, m, *_: (m[2 + first_chunk + i], 0)),
                pl.BlockSpec((rows, at_once * DV), lambda i, p, m, *_: (m[2 + first_chunk + i], p)),
            ]
            + [VMEM_SPEC] * len(pools)
            + [pl.BlockSpec(memory_space=pl.ANY)],
            out_specs=[VMEM_SPEC] * len(outs),
            scratch_shapes=[
                pltpu.VMEM((PICKS * KBLK, 256), BF16),
                pltpu.VMEM((256, PICKS * KBLK), BF16),
                pltpu.VMEM((256, PICKS * KBLK), BF16),
                pltpu.VMEM((PICKS * KBLK, 256), BF16),
                pltpu.VMEM((steps, rows, at_once * DV), BF16),
                pltpu.VMEM(out_weight.shape, BF16),
                pltpu.SemaphoreType.DMA,
            ],
        ),
        out_shape=outs,
        compiler_params=pltpu.CompilerParams(vmem_limit_bytes=CHOSEN_LIMIT),
        cost_estimate=pl.CostEstimate(
            flops=rows * heads * PICKS * KBLK * 64,
            bytes_accessed=out_weight.size,
            transcendentals=0,
        ),
        name="chosen_and_project",
    )(meta, slots, dead, queries, gates, near, *pools, out_weight)


VMEM_SPEC = pl.BlockSpec(memory_space=pltpu.VMEM)


def single_step(kernel, name, scalars, arrays, outs, scratch=(), in_spec=None, out_spec=None):
    whole = lambda x: pl.BlockSpec(x.shape, lambda i, *_: (0,) * len(x.shape))
    return pl.pallas_call(
        kernel,
        grid_spec=pltpu.PrefetchScalarGridSpec(
            num_scalar_prefetch=len(scalars),
            grid=(1,),
            in_specs=[in_spec or whole(x) for x in arrays],
            out_specs=[out_spec or whole(x) for x in outs],
            scratch_shapes=list(scratch),
        ),
        out_shape=outs,
        compiler_params=pltpu.CompilerParams(vmem_limit_bytes=VMEM_LIMIT),
        name=name,
    )(*scalars, *arrays)


def last_sum(halves, rows, kept_ref, *refs):
    halves, others, out_ref = refs[:halves], refs[halves:-1], refs[-1]
    at = pl.ds(pl.multiple_of(pl.program_id(0) * rows, rows), rows)
    first = 0
    for half in halves:
        cols = slice(first, first + half.shape[1])
        total = kept_ref[at, cols].astype(F32) + half[at].astype(F32)
        for other in others:
            total = total + other[at, cols].astype(F32)
        out_ref[:, cols] = total.astype(BF16)
        first += half.shape[1]


def local(
    queries,
    key_rows,
    value_rows,
    comp_key_weight,
    comp_value_weight,
    block_picks,
    gate_logits,
    out_weight,
):
    tokens = queries.shape[0]
    heads = queries.shape[1] // QK
    n_ctx, n_head = lax.axis_size("ctx"), lax.axis_size("head")
    shard, head_at = lax.axis_index("ctx"), lax.axis_index("head")
    group = head_at * heads // (HEADS // GROUPS)
    per_owner = tokens // KBLK
    lists = tokens // QBLK
    folds = tokens // CBLK
    groups = n_ctx // 2
    rim_blocks = WINDOW // KBLK
    packed_rows = per_owner * BROWS
    bf16 = lambda *shape: jax.ShapeDtypeStruct(shape, BF16)

    chips = n_head // 2
    chip, core = head_at // 2, lax.rem(head_at, 2)
    order = []
    for step in list(range(1, chips)) + [0]:
        target = lax.rem(chip + step, chips) * 2
        order += [target + 1 - core, target + core]
    where = jnp.stack([group, shard, shard * tokens] + order).astype(jnp.int32)
    rim_rows = rim_blocks * BROWS
    fold_weights = jnp.concatenate([comp_key_weight, comp_value_weight], axis=1)
    int32 = lambda *shape: jax.ShapeDtypeStruct(shape, jnp.int32)
    prep_out = [bf16(packed_rows + 3 * folds, 128), bf16(rim_rows, 128)]
    prep_out += [int32(1, n_ctx * lists), int32(lists, 2 * PICKS), int32(lists, 2 * PICKS)]
    prep_out += [bf16(256, tokens)] * 2 + [bf16(tokens, 256)]
    packed, rim, named, slots, dead, even, odd, val = pl.pallas_call(
        prep_kernel,
        grid_spec=pltpu.PrefetchScalarGridSpec(
            num_scalar_prefetch=1,
            grid=(1,),
            in_specs=[pl.BlockSpec(memory_space=pl.ANY)] * 4,
            out_specs=[VMEM_SPEC] * 2
            + [pl.BlockSpec(x.shape, lambda i, g: (0, 0)) for x in prep_out[2:5]]
            + [VMEM_SPEC] * 3,
            scratch_shapes=[
                pltpu.VMEM(block_picks.shape, jnp.int32),
                pltpu.VMEM((tokens, PAIR), BF16),
                pltpu.VMEM((tokens, DV), BF16),
                pltpu.VMEM((CBLK, PAIR), F32),
                pltpu.VMEM((CBLK, DV), F32),
                pltpu.SemaphoreType.DMA((5,)),
            ],
        ),
        out_shape=prep_out,
        compiler_params=pltpu.CompilerParams(vmem_limit_bytes=51 * 1024 * 1024),
        name="prep",
    )(where, block_picks, key_rows, value_rows, fold_weights)
    other = lax.ppermute(packed, "ctx", [(i, i ^ 1) for i in range(n_ctx)])
    named = [named] + [
        lax.ppermute(named, "ctx", [(i, i - 2 * d) for i in range(2 * d, n_ctx)])
        for d in range(1, groups)
    ]
    far_rim = lax.ppermute(rim, "ctx", [(i, i + 1) for i in range(1, n_ctx - 1, 2)])

    gates = jax.nn.sigmoid(gate_logits).reshape(tokens, 3 * heads)
    gates = jnp.pad(gates, ((0, 0), (0, 128 - 3 * heads)))
    sent = bf16(lists * BROWS + 3 * folds, 128)

    def pack(beside, lists_in, rows):
        return single_step(
            functools.partial(pack_kernel, lists, beside),
            "pack",
            [where, *lists_in],
            [rows],
            [sent] * len(lists_in),
            in_spec=VMEM_SPEC,
            out_spec=VMEM_SPEC,
        )

    def all_ahead(sends):
        moved = []
        for distance, send in reversed(list(enumerate(sends, 1))):
            route = [(i, i + 2 * distance) for i in range(n_ctx - 2 * distance)]
            moved.append(lax.ppermute(send, "ctx", route))
        return moved[::-1]

    named, gates = lax.optimization_barrier((named, gates))
    own_sends = pack(False, named[1:], packed)
    own_sends, even = lax.optimization_barrier((own_sends, even))
    from_same = all_ahead(own_sends)

    reach = WINDOW // QBLK
    near = functools.partial(near_branch, where=where, queries=queries, gates=gates)
    near = functools.partial(near, keys=(even, odd, val))
    mixed = near(reach, lists - reach, rims=None, prior=None)

    other, mixed = lax.optimization_barrier((other, mixed))
    beside, *other_sends = pack(True, named, other)
    from_other = all_ahead(other_sends)
    mixed = near(0, reach, rims=(other, far_rim), prior=mixed)

    farthest_first = reversed(list(zip(from_same, from_other)))
    received = [beside] + [x for both in farthest_first for x in both]
    pools = single_step(
        functools.partial(pool_kernel, groups, lists),
        "pool",
        [where],
        [packed] + received,
        [bf16(n_ctx * lists * KBLK, 256), bf16(n_ctx * lists * KBLK, DV)]
        + [bf16(256, n_ctx * folds)] * 2
        + [bf16(n_ctx * folds, 256)],
        [pltpu.VMEM((n_ctx * folds, 256), BF16)],
        in_spec=VMEM_SPEC,
        out_spec=VMEM_SPEC,
    )
    rows = tokens // n_head
    across = [(i, i ^ 1) for i in range(n_head)]

    model = out_weight.shape[1]

    def project(first_chunk, widths):
        return chosen_and_project(
            first_chunk, widths, rows, where, slots, dead, queries, gates, mixed, pools, out_weight
        )

    sums = []
    for step in range(chips - 1):
        other = lax.ppermute(project(1 + 2 * step, [[model]])[0], "head", across)
        mine = project(2 + 2 * step, [[model]])[0]
        summed = (mine.astype(F32) + other.astype(F32)).astype(BF16)
        summed, where = lax.optimization_barrier((summed, where))
        sums.append(summed)
    *passed, kept = project(n_head - 1, [[model // 2] * 2, [model]])
    near_parts = [lax.ppermute(x, "head", across) for x in passed]
    arrived = []
    for step, summed in enumerate(sums, 1):
        route = [(i, (i + 2 * step) % n_head) for i in range(n_head)]
        arrived.append(lax.ppermute(summed, "head", route))
    steps = 4 if rows % 64 == 0 else 1
    row_block = pl.BlockSpec((rows // steps, model), lambda i: (i, 0))
    return pl.pallas_call(
        functools.partial(last_sum, len(near_parts), rows // steps),
        grid=(steps,),
        in_specs=[VMEM_SPEC] * (1 + len(near_parts) + len(arrived)),
        out_specs=row_block,
        out_shape=bf16(rows, model),
        compiler_params=pltpu.CompilerParams(vmem_limit_bytes=VMEM_LIMIT),
        name="last_sum",
    )(kept, *near_parts, *arrived)


def solution(mesh):
    placed = (
        P("ctx", "head"),
        P("ctx", None),
        P("ctx", None),
        P(),
        P(),
        P("ctx", None, None),
        P("ctx", None, "head"),
        P("head", None),
    )
    return jax.shard_map(
        local, mesh=mesh, in_specs=placed, out_specs=P(("ctx", "head"), None), check_vma=False
    )
```

profile of v0, /device:TPU:5, one launch (start us, length us, event | category | flops | bytes accessed | tf_op | source)
XLA Modules:
  0.0 174.0 jit_solution(3266471166669757298)
XLA Ops:
  0.0 0.9 pad_maximum_fusion.fold_in
  0.9 0.1 stack.31.where_ref.refs_0_
  1.0 0.7 copy-done
  1.7 3.2 %prep.1 = (bf16[2656,128]{1,0:T(8,128)(2,1)S(1)}, bf16[1280,128]{1,0:T(8,128)(2,1)}, s32[1,32]{1,0:T(1,128)S(1)}, s32[4,32]{1,0:T(4,128)S(1)}, s32[4,32]{1,0:T(4...) custom-call(s32[7]{0:T(128)S(1)} %stack.31.where_ref.refs_0_, ...), custom_call_target="tpu_custom_call" | custom-call | tf_op jit(solution)/shard_map/prep/pallas_call | solution.py:666
  5.0 1.3 collective-permute-start.2
  6.3 1.3 collective-permute-start.1
  7.6 1.3 collective-permute-start
  8.9 5.2 %collective-permute-start.4 = (bf16[1280,128]{1,0:T(8,128)(2,1)}, bf16[1280,128]{1,0:T(8,128)(2,1)S(1)}, u32[]{:S(2)}, u32[]{:S(2)}) collective-permute-start(bf16[1280,128]{1,0:T(8,128)(2,1)} %get-tuple-element.57), channel_id=1, source_target_pairs={{4,8},{12,16},{20,24},{5,9},{13,17},{21,25},{6,10},{14,18},{22,26}... | collective-permute-start | bytes 983048 | tf_op jit(solution)/shard_map/ppermute | solution.py:693
  14.2 1.0 copy.11
  15.2 1.1 pad.4.gate_ref.refs_4_
  16.3 0.6 pack.2
  16.9 2.2 %collective-permute-start.5 = (bf16[736,128]{1,0:T(8,128)(2,1)S(1)}, bf16[736,128]{1,0:T(8,128)(2,1)S(1)}, u32[]{:S(2)}, u32[]{:S(2)}) collective-permute-start(bf16[736,128]{1,0:T(8,128)(2,1)S(1)} %get-tuple-element.61), channel_id=1, source_target_pairs={{0,24},{4,28},{1,25},{5,29},{2,26},{6,30},{3,27},{7,31}} | collective-permute-start | bytes 565256 | tf_op jit(solution)/shard_map/ppermute | solution.py:714
  19.1 3.4 %collective-permute-start.7 = (bf16[736,128]{1,0:T(8,128)(2,1)S(1)}, bf16[736,128]{1,0:T(8,128)(2,1)S(1)}, u32[]{:S(2)}, u32[]{:S(2)}) collective-permute-start(bf16[736,128]{1,0:T(8,128)(2,1)S(1)} %get-tuple-element.63), channel_id=1, source_target_pairs={{0,16},{4,20},{8,24},{12,28},{1,17},{5,21},{9,25},{13,29},{2,18},{... | collective-permute-start | bytes 565256 | tf_op jit(solution)/shard_map/ppermute | solution.py:714
  22.5 1.3 collective-permute-start.9
  23.8 25.7 %near_branch.2.refs_5_ = bf16[1024,2048]{1,0:T(8,128)(2,1)} custom-call(s32[7]{0:T(128)S(1)} %stack.31.where_ref.refs_0_, bf16[1024,3072]{1,0:T(8,128)(2,1)} %refs_3_.5, f32[1024,128]{1,0:T(8,128)S(1)} %pad.4.gate_ref.refs_4_, bf16[256,1024]{1,0:T(8,128)(2,1)S(1)} %get-tuple-element.53.refs_0_, bf16[256,1024]{1,0:T(8,128)(2,1)S(1)} %get-tuple-element.54.refs_1_, ...), custom_call_target="tpu_custom_call" | custom-call | flops 402653184 | bytes 7340032 | tf_op jit(solution)/shard_map/near_branch/pallas_call | solution.py:444
  49.5 0.6 pack.3
  50.2 1.3 collective-permute-start.6
  51.5 1.3 collective-permute-start.8
  52.8 1.6 collective-permute-start.10
  54.3 18.6 %near_branch.3.refs_5_ = bf16[1024,2048]{1,0:T(8,128)(2,1)} custom-call(s32[7]{0:T(128)S(1)} %stack.31.where_ref.refs_0_, bf16[1024,3072]{1,0:T(8,128)(2,1)} %refs_3_.5, f32[1024,128]{1,0:T(8,128)S(1)} %pad.4.gate_ref.refs_4_, bf16[256,1024]{1,0:T(8,128)(2,1)S(1)} %get-tuple-element.53.refs_0_, ...), custom_call_target="tpu_custom_call", output_to_operand_aliasing={{}: (8, {})} | custom-call | flops 402653184 | bytes 7340032 | tf_op jit(solution)/shard_map/near_branch/pallas_call | solution.py:444
  73.0 1.2 pool.1
  74.2 23.0 %chosen_and_project.4 = bf16[256,2560]{1,0:T(8,128)(2,1)S(1)} custom-call(s32[7]{0:T(128)S(1)} %stack.31.where_ref.refs_0_, s32[4,32]{1,0:T(4,128)S(1)} %get-tuple-element.41.refs_1_, s32[4,32]{1,0:T(4,128)S(1)} %get-tuple-element.42.refs_2_, bf16[1024,3072]{1,0:T(8,128)(2,1)} %refs_3_.5, f32[1024,128]{1,0:T(8,128)S(1)} %pad.4.gate_ref.refs_4_, ...), custom_call_target="tpu_custom_call" | custom-call | flops 268435456 | bytes 5242880 | tf_op jit(solution)/shard_map/chosen_and_project/pallas_call | solution.py:563
  97.2 2.4 %collective-permute-start.11 = (bf16[256,2560]{1,0:T(8,128)(2,1)S(1)}, bf16[256,2560]{1,0:T(8,128)(2,1)S(1)}, u32[]{:S(2)}, u32[]{:S(2)}) collective-permute-start(bf16[256,2560]{1,0:T(8,128)(2,1)S(1)} %chosen_and_project.4), channel_id=1, source_target_pairs={{0,1},{1,0},{2,3},{3,2},{4,5},{5,4},{6,7},{7,6},{8,9},{9,8},{10,11... | collective-permute-start | bytes 3932168 | tf_op jit(solution)/shard_map/ppermute | solution.py:758
  99.7 23.2 %chosen_and_project.3 = bf16[256,2560]{1,0:T(8,128)(2,1)S(1)} custom-call(s32[7]{0:T(128)S(1)} %stack.31.where_ref.refs_0_, s32[4,32]{1,0:T(4,128)S(1)} %get-tuple-element.41.refs_1_, s32[4,32]{1,0:T(4,128)S(1)} %get-tuple-element.42.refs_2_, bf16[1024,3072]{1,0:T(8,128)(2,1)} %refs_3_.5, f32[1024,128]{1,0:T(8,128)S(1)} %pad.4.gate_ref.refs_4_, ...), custom_call_target="tpu_custom_call" | custom-call | flops 268435456 | bytes 5242880 | tf_op jit(solution)/shard_map/chosen_and_project/pallas_call | solution.py:563
  122.9 0.3 add_convert_fusion
  123.2 1.3 collective-permute-start.14
  124.5 44.5 %chosen_and_project.5 = (bf16[256,1280]{1,0:T(8,128)(2,1)S(1)}, bf16[256,1280]{1,0:T(8,128)(2,1)S(1)}, bf16[256,2560]{1,0:T(8,128)(2,1)S(1)}) custom-call(s32[7]{0:T(128)S(1)} %stack.31.where_ref.refs_0_, s32[4,32]{1,0:T(4,128)S(1)} %get-tuple-element.41.refs_1_, s32[4,32]{1,0:T(4,128)S(1)} %get-tuple-element.42.refs_2_, bf16[1024,3072]{1,0:T(8,128)(2,1)} %refs_3_.5, ...), custom_call_target="tpu_custom_call" | custom-call | flops 268435456 | bytes 5242880 | tf_op jit(solution)/shard_map/chosen_and_project/pallas_call | solution.py:563
  169.0 0.4 collective-permute-start.12
  169.4 0.2 collective-permute-start.13
  169.6 1.6 collective-permute-done.12.refs_0_
  171.2 0.9 collective-permute-done.13.refs_1_
  172.1 1.8 %last_sum.1 = bf16[256,2560]{1,0:T(8,128)(2,1)} custom-call(bf16[256,2560]{1,0:T(8,128)(2,1)S(1)} %get-tuple-element.73.kept_ref, bf16[256,1280]{1,0:T(8,128)(2,1)S(1)} %collective-permute-done.12.refs_0_, bf16[256,1280]{1,0:T(8,128)(2,1)S(1)} %collective-permute-done.13.refs_1_, bf16[256,2560]{1,0:T(8,128)(2,1)S(1)} %collective-permute-done.14.refs_2_), custom_call_target="tpu_custom_call" | custom-call | tf_op jit(solution)/shard_map/last_sum/pallas_call | solution.py:771
  (18 shorter events, 0.2 us)
Async XLA Ops:
  1.0 0.7 copy-start
  1.7 12.3 %copy-start.1 = (f32[1024,3,16]{0,2,1:T(8,128)S(1)}, f32[1024,3,16]{0,2,1:T(8,128)}, u32[]{:S(2)}) copy-start(f32[1024,3,16]{0,2,1:T(8,128)} %param.14) | copy-start | bytes 589828
  4.9 44.6 %collective-permute-start.3 = (bf16[2656,128]{1,0:T(8,128)(2,1)S(1)}, bf16[2656,128]{1,0:T(8,128)(2,1)S(1)}, u32[]{:S(2)}, u32[]{:S(2)}) collective-permute-start(bf16[2656,128]{1,0:T(8,128)(2,1)S(1)} %get-tuple-element.48.refs_3_.own_ref), channel_id=1, source_target_pairs={{0,4},{4,0},{8,12},{12,8},{16,20},{20,16},{24,28},{28,24},{1,5},{5... | collective-permute-start | bytes 2039816 | tf_op jit(solution)/shard_map/ppermute | solution.py:688
  5.0 11.2 %collective-permute-start.2 = (s32[1,32]{1,0:T(1,128)S(1)}, s32[1,32]{1,0:T(1,128)S(1)}, u32[]{:S(2)}, u32[]{:S(2)}) collective-permute-start(s32[1,32]{1,0:T(1,128)S(1)} %get-tuple-element.59.refs_0_), channel_id=1, source_target_pairs={{24,0},{28,4},{25,1},{29,5},{26,2},{30,6},{27,3},{31,7}} | collective-permute-start | bytes 392 | tf_op jit(solution)/shard_map/ppermute | solution.py:690
  6.3 9.9 %collective-permute-start.1 = (s32[1,32]{1,0:T(1,128)S(1)}, s32[1,32]{1,0:T(1,128)S(1)}, u32[]{:S(2)}, u32[]{:S(2)}) collective-permute-start(s32[1,32]{1,0:T(1,128)S(1)} %get-tuple-element.59.refs_0_), channel_id=1, source_target_pairs={{16,0},{20,4},{24,8},{28,12},{17,1},{21,5},{25,9},{29,13},{18,2},{... | collective-permute-start | bytes 392 | tf_op jit(solution)/shard_map/ppermute | solution.py:690
  7.6 8.7 %collective-permute-start = (s32[1,32]{1,0:T(1,128)S(1)}, s32[1,32]{1,0:T(1,128)S(1)}, u32[]{:S(2)}, u32[]{:S(2)}) collective-permute-start(s32[1,32]{1,0:T(1,128)S(1)} %get-tuple-element.59.refs_0_), channel_id=1, source_target_pairs={{8,0},{12,4},{16,8},{20,12},{24,16},{28,20},{9,1},{13,5},{17,9},{2... | collective-permute-start | bytes 392 | tf_op jit(solution)/shard_map/ppermute | solution.py:690
  8.9 43.9 %collective-permute-start.4 = (bf16[1280,128]{1,0:T(8,128)(2,1)}, bf16[1280,128]{1,0:T(8,128)(2,1)S(1)}, u32[]{:S(2)}, u32[]{:S(2)}) collective-permute-start(bf16[1280,128]{1,0:T(8,128)(2,1)} %get-tuple-element.57), channel_id=1, source_target_pairs={{4,8},{12,16},{20,24},{5,9},{13,17},{21,25},{6,10},{14,18},{22,26}... | collective-permute-start | bytes 983048 | tf_op jit(solution)/shard_map/ppermute | solution.py:693
  16.9 34.6 %collective-permute-start.5 = (bf16[736,128]{1,0:T(8,128)(2,1)S(1)}, bf16[736,128]{1,0:T(8,128)(2,1)S(1)}, u32[]{:S(2)}, u32[]{:S(2)}) collective-permute-start(bf16[736,128]{1,0:T(8,128)(2,1)S(1)} %get-tuple-element.61), channel_id=1, source_target_pairs={{0,24},{4,28},{1,25},{5,29},{2,26},{6,30},{3,27},{7,31}} | collective-permute-start | bytes 565256 | tf_op jit(solution)/shard_map/ppermute | solution.py:714
  19.1 53.9 %collective-permute-start.7 = (bf16[736,128]{1,0:T(8,128)(2,1)S(1)}, bf16[736,128]{1,0:T(8,128)(2,1)S(1)}, u32[]{:S(2)}, u32[]{:S(2)}) collective-permute-start(bf16[736,128]{1,0:T(8,128)(2,1)S(1)} %get-tuple-element.63), channel_id=1, source_target_pairs={{0,16},{4,20},{8,24},{12,28},{1,17},{5,21},{9,25},{13,29},{2,18},{... | collective-permute-start | bytes 565256 | tf_op jit(solution)/shard_map/ppermute | solution.py:714
  22.5 50.5 %collective-permute-start.9 = (bf16[736,128]{1,0:T(8,128)(2,1)S(1)}, bf16[736,128]{1,0:T(8,128)(2,1)S(1)}, u32[]{:S(2)}, u32[]{:S(2)}) collective-permute-start(bf16[736,128]{1,0:T(8,128)(2,1)S(1)} %get-tuple-element.65), channel_id=1, source_target_pairs={{0,8},{4,12},{8,16},{12,20},{16,24},{20,28},{1,9},{5,13},{9,17},{1... | collective-permute-start | bytes 565256 | tf_op jit(solution)/shard_map/ppermute | solution.py:714
  50.2 22.8 %collective-permute-start.6 = (bf16[736,128]{1,0:T(8,128)(2,1)S(1)}, bf16[736,128]{1,0:T(8,128)(2,1)S(1)}, u32[]{:S(2)}, u32[]{:S(2)}) collective-permute-start(bf16[736,128]{1,0:T(8,128)(2,1)S(1)} %get-tuple-element.62), channel_id=1, source_target_pairs={{0,24},{4,28},{1,25},{5,29},{2,26},{6,30},{3,27},{7,31}} | collective-permute-start | bytes 565256 | tf_op jit(solution)/shard_map/ppermute | solution.py:714
  51.5 21.5 %collective-permute-start.8 = (bf16[736,128]{1,0:T(8,128)(2,1)S(1)}, bf16[736,128]{1,0:T(8,128)(2,1)S(1)}, u32[]{:S(2)}, u32[]{:S(2)}) collective-permute-start(bf16[736,128]{1,0:T(8,128)(2,1)S(1)} %get-tuple-element.64), channel_id=1, source_target_pairs={{0,16},{4,20},{8,24},{12,28},{1,17},{5,21},{9,25},{13,29},{2,18},{... | collective-permute-start | bytes 565256 | tf_op jit(solution)/shard_map/ppermute | solution.py:714
  52.8 20.2 %collective-permute-start.10 = (bf16[736,128]{1,0:T(8,128)(2,1)S(1)}, bf16[736,128]{1,0:T(8,128)(2,1)S(1)}, u32[]{:S(2)}, u32[]{:S(2)}) collective-permute-start(bf16[736,128]{1,0:T(8,128)(2,1)S(1)} %get-tuple-element.66), channel_id=1, source_target_pairs={{0,8},{4,12},{8,16},{12,20},{16,24},{20,28},{1,9},{5,13},{9,17},{1... | collective-permute-start | bytes 565256 | tf_op jit(solution)/shard_map/ppermute | solution.py:714
  97.2 25.7 %collective-permute-start.11 = (bf16[256,2560]{1,0:T(8,128)(2,1)S(1)}, bf16[256,2560]{1,0:T(8,128)(2,1)S(1)}, u32[]{:S(2)}, u32[]{:S(2)}) collective-permute-start(bf16[256,2560]{1,0:T(8,128)(2,1)S(1)} %chosen_and_project.4), channel_id=1, source_target_pairs={{0,1},{1,0},{2,3},{3,2},{4,5},{5,4},{6,7},{7,6},{8,9},{9,8},{10,11... | collective-permute-start | bytes 3932168 | tf_op jit(solution)/shard_map/ppermute | solution.py:758
  123.2 48.9 %collective-permute-start.14 = (bf16[256,2560]{1,0:T(8,128)(2,1)S(1)}, bf16[256,2560]{1,0:T(8,128)(2,1)S(1)}, u32[]{:S(2)}, u32[]{:S(2)}) collective-permute-start(bf16[256,2560]{1,0:T(8,128)(2,1)S(1)} %add_convert_fusion), channel_id=1, source_target_pairs={{0,2},{1,3},{2,0},{3,1},{4,6},{5,7},{6,4},{7,5},{8,10},{9,11},{10,... | collective-permute-start | bytes 3932168 | tf_op jit(solution)/shard_map/ppermute | solution.py:768
  169.0 2.2 %collective-permute-start.12 = (bf16[256,1280]{1,0:T(8,128)(2,1)S(1)}, bf16[256,1280]{1,0:T(8,128)(2,1)S(1)}, u32[]{:S(2)}, u32[]{:S(2)}) collective-permute-start(bf16[256,1280]{1,0:T(8,128)(2,1)S(1)} %get-tuple-element.74), channel_id=1, source_target_pairs={{0,1},{1,0},{2,3},{3,2},{4,5},{5,4},{6,7},{7,6},{8,9},{9,8},{10,11... | collective-permute-start | bytes 1966088 | tf_op jit(solution)/shard_map/ppermute | solution.py:764
  169.4 2.7 %collective-permute-start.13 = (bf16[256,1280]{1,0:T(8,128)(2,1)S(1)}, bf16[256,1280]{1,0:T(8,128)(2,1)S(1)}, u32[]{:S(2)}, u32[]{:S(2)}) collective-permute-start(bf16[256,1280]{1,0:T(8,128)(2,1)S(1)} %get-tuple-element.75), channel_id=1, source_target_pairs={{0,1},{1,0},{2,3},{3,2},{4,5},{5,4},{6,7},{7,6},{8,9},{9,8},{10,11... | collective-permute-start | bytes 1966088 | tf_op jit(solution)/shard_map/ppermute | solution.py:764
where the time goes:
time: 175 us; the launch traced here: 174 us
  Pallas kernels  143 us (82%)
  starting transfers between devices  24.4 us (14%)
  local copies, waits for them, and re-layouts  2.87 us (2%)
  waiting for transfers between devices  2.56 us (1%)
    pallas_call x3, Pallas kernels, chosen_and_project(): pl.pallas_call(functools.partial(chosen_kernel, heads, (first_chunk, widt...  90.8 us
    pallas_call x2, Pallas kernels, near_branch(): pl.pallas_call(functools.partial(near_kernel, heads, first_block, rims is...  44.4 us
    ppermute x6, starting transfers between devices, all_ahead(): moved.append(lax.ppermute(send, 'ctx', route))  11 us
    ppermute x1, starting transfers between devices, local(): lax.ppermute(rim, 'ctx', [(i, i + 1) for i in range(1, n_ctx - 1, 2)])  5.16 us
    ppermute x3, starting transfers between devices, local(): lax.ppermute(named, 'ctx', [(i, i - 2 * d) for i in range(2 * d, n_ctx)])  3.88 us
  transfers between devices with their start and end apart: 15, of which 2 were waited for; matrix products, arithmetic and copies ran while one was open for 1% of the time, Pallas kernels for 65%

commit v1 on v0

--- a/solution.py
+++ b/solution.py
@@ -295,6 +295,28 @@
     return scores if mask is None else mask(scores)
 
 
+def plain_weights(scores):
+    return jnp.exp2(scores * SCALE).astype(BF16)
+
+
+def corner_weights(scores, later):
+    half = QBLK // 2
+    row, col = iota(half, half, 0), iota(half, half, 1)
+    keep = col >= row if later else col <= row
+    none = jnp.zeros((half, half), BF16)
+    pieces = []
+    for first in range(0, scores.shape[0], QBLK):
+        for lower_half in range(2):
+            rows = scores[first + lower_half * half : first + (lower_half + 1) * half]
+            parts = [rows[:, :half], rows[:, half:]]
+            parts[lower_half] = plain_weights(jnp.where(keep, parts[lower_half], NEG))
+            other = 1 - lower_half
+            full = (lower_half == 0) == later
+            parts[other] = plain_weights(parts[other]) if full else none
+            pieces.append(jnp.concatenate(parts, axis=1))
+    return jnp.concatenate(pieces, axis=0)
+
+
 def in_range(total):
     good = jnp.where((total >= LOW_TOTAL) & (total <= HIGH_TOTAL), 1.0, 0.0)
     return jnp.min(good.reshape(-1, 8, DV), axis=0)
@@ -313,11 +335,11 @@
         fresh, parts = [], []
         for at, (tiles, values) in enumerate(branches):
             weights, ahead = [], []
-            for place, (keys, mask) in enumerate(tiles):
+            for place, (keys, mask, weigh) in enumerate(tiles):
                 if q is not None:
-                    ahead.append(scores_of(q, keys(unit[1]), mask))
+                    ahead.append(scores_of(q, keys(unit[1]), mask if weigh is None else None))
                 if held is not None:
-                    weights.append(jnp.exp2(held[at][place] * SCALE).astype(BF16))
+                    weights.append((weigh or plain_weights)(held[at][place]))
             fresh.append(ahead)
             parts.append((weights, values))
         if held is not None:
@@ -332,7 +354,7 @@
                 q = load(pair, side, 1)
                 parts = []
                 for tiles, values in branches:
-                    scores = [scores_of(q, keys(side), mask) for keys, mask in tiles]
+                    scores = [scores_of(q, keys(side), mask) for keys, mask, _ in tiles]
                     scores = jnp.concatenate(scores, axis=1)
                     top = jnp.max(scores, axis=1, keepdims=True)
                     shifted = (scores - jnp.maximum(top, -1e28)) * SCALE
@@ -359,8 +381,9 @@
     return pl.ds(aligned(pair * 2 * DV + side * DV), DV)
 
 
-def gate_loader(gate_ref, first, heads):
-    turned = pltpu.roll(gate_ref[...], lax.rem(128 - first, 128), 1)
+def gate_loader(gate_ref, wide, first, heads):
+    wide[:, : gate_ref.shape[1]] = jax.nn.sigmoid(gate_ref[...])
+    turned = pltpu.roll(wide[...], lax.rem(128 - first, 128), 1)
 
     def load(pair, side, n, branch):
         if isinstance(pair, int):
@@ -383,6 +406,7 @@
 
 
 def near_kernel(heads, first_block, rim, where_ref, q_ref, gate_ref, *refs):
+    *refs, wide = refs
     keys = refs[:3]
     if rim:
         out_ref, ext = refs[-4], refs[-3:]
@@ -395,12 +419,12 @@
     else:
         out_ref, reach = refs[-1], WINDOW
     count = q_ref.shape[1] // QK
-    gate = gate_loader(gate_ref, pl.program_id(1) * count, heads)
+    gate = gate_loader(gate_ref, wide, pl.program_id(1) * count, heads)
     base = pl.multiple_of((first_block + pl.program_id(0)) * QBLK - reach, QBLK)
     row, col = iota(QBLK, QBLK, 0), iota(QBLK, QBLK, 1)
 
-    def tile(place, mask):
-        return (lambda side: keys[side][:, pl.ds(base + place * QBLK, QBLK)]), mask
+    def tile(place, mask, weigh):
+        return (lambda side: keys[side][:, pl.ds(base + place * QBLK, QBLK)]), mask, weigh
 
     def finish(pair, side, n, parts):
         ((num, den),) = parts
@@ -411,9 +435,17 @@
         return [den]
 
     tiles = [
-        tile(0, lambda x: jnp.where(repeated(col >= row, x.shape[0]), x, NEG)),
-        tile(1, None),
-        tile(2, lambda x: jnp.where(repeated(col <= row, x.shape[0]), x, NEG)),
+        tile(
+            0,
+            lambda x: jnp.where(repeated(col >= row, x.shape[0]), x, NEG),
+            lambda x: corner_weights(x, True),
+        ),
+        tile(1, None, None),
+        tile(
+            2,
+            lambda x: jnp.where(repeated(col <= row, x.shape[0]), x, NEG),
+            lambda x: corner_weights(x, False),
+        ),
     ]
     values = lambda: keys[2][pl.ds(base, WINDOW + QBLK)]
     over_heads(count // 2, query_loader(q_ref), [(tiles, values)], finish)
@@ -427,7 +459,7 @@
     operands = [queries, gates, *keys]
     specs = [
         pl.BlockSpec((QBLK, at_once * QK), row_block),
-        pl.BlockSpec((QBLK, 128), lambda i, p, *_: (i + first_block, 0)),
+        pl.BlockSpec((QBLK, 3 * heads), lambda i, p, *_: (i + first_block, 0)),
     ]
     specs += [VMEM_SPEC] * len(keys)
     alias, scratch = {}, []
@@ -448,7 +480,7 @@
             grid=(block_count, heads // at_once),
             in_specs=specs,
             out_specs=pl.BlockSpec((QBLK, at_once * DV), row_block),
-            scratch_shapes=scratch,
+            scratch_shapes=scratch + [pltpu.VMEM((QBLK, 128), F32)],
         ),
         out_shape=jax.ShapeDtypeStruct((tokens, heads * DV), BF16),
         input_output_aliases=alias,
@@ -468,7 +500,7 @@
     meta_ref, slots_ref, dead_ref, q_ref, gate_ref, near_ref = refs[:6]
     (key_pool, val_pool), cfold, weight_ref = refs[6:8], refs[8:11], refs[11]
     outs = list(refs[12 : 12 + out_count])
-    gathered, even, odd, val, attended, weight, weight_sem = refs[12 + out_count :]
+    gathered, even, odd, val, attended, weight, weight_sem, wide = refs[12 + out_count :]
     keys = (even, odd)
     turn, step = pl.program_id(0), pl.program_id(1)
     last = pl.num_programs(1) - 1
@@ -500,7 +532,7 @@
     def _():
         copy.start()
 
-    gate = gate_loader(gate_ref, step * count, heads)
+    gate = gate_loader(gate_ref, wide, step * count, heads)
     row = iota(rows, TILE, 0)
     col = iota(rows, TILE, 1)
     own_keep = (col >= KBLK) | (col <= row + first_row)
@@ -514,7 +546,7 @@
         return lambda x: jnp.where(repeated(ends <= row + position, x.shape[0]), x, NEG)
 
     def tile(refs, place, mask):
-        return (lambda side: refs[side][:, place * TILE : (place + 1) * TILE]), mask
+        return (lambda side: refs[side][:, place * TILE : (place + 1) * TILE]), mask, None
 
     chosen = [tile(keys, p, own_mask if p == 0 else None) for p in range(PICKS * KBLK // TILE)]
     folded = [tile(cfold, p, comp_mask(p)) for p in range(cfold[2].shape[0] // TILE)]
@@ -567,7 +599,7 @@
             grid=(len(widths), steps),
             in_specs=[
                 pl.BlockSpec((rows, at_once * QK), lambda i, p, m, *_: (m[2 + first_chunk + i], p)),
-                pl.BlockSpec((rows, 128), lambda i, p, m, *_: (m[2 + first_chunk + i], 0)),
+                pl.BlockSpec((rows, 3 * heads), lambda i, p, m, *_: (m[2 + first_chunk + i], 0)),
                 pl.BlockSpec((rows, at_once * DV), lambda i, p, m, *_: (m[2 + first_chunk + i], p)),
             ]
             + [VMEM_SPEC] * len(pools)
@@ -581,6 +613,7 @@
                 pltpu.VMEM((steps, rows, at_once * DV), BF16),
                 pltpu.VMEM(out_weight.shape, BF16),
                 pltpu.SemaphoreType.DMA,
+                pltpu.VMEM((rows, 128), F32),
             ],
         ),
         out_shape=outs,
@@ -690,10 +723,8 @@
         lax.ppermute(named, "ctx", [(i, i - 2 * d) for i in range(2 * d, n_ctx)])
         for d in range(1, groups)
     ]
-    far_rim = lax.ppermute(rim, "ctx", [(i, i + 1) for i in range(1, n_ctx - 1, 2)])
-
-    gates = jax.nn.sigmoid(gate_logits).reshape(tokens, 3 * heads)
-    gates = jnp.pad(gates, ((0, 0), (0, 128 - 3 * heads)))
+
+    gates = gate_logits.reshape(tokens, 3 * heads)
     sent = bf16(lists * BROWS + 3 * folds, 128)
 
     def pack(beside, lists_in, rows):
@@ -714,7 +745,8 @@
             moved.append(lax.ppermute(send, "ctx", route))
         return moved[::-1]
 
-    named, gates = lax.optimization_barrier((named, gates))
+    named, gates, rim = lax.optimization_barrier((named, gates, rim))
+    far_rim = lax.ppermute(rim, "ctx", [(i, i + 1) for i in range(1, n_ctx - 1, 2)])
     own_sends = pack(False, named[1:], packed)
     own_sends, even = lax.optimization_barrier((own_sends, even))
     from_same = all_ahead(own_sends)
@@ -766,7 +798,7 @@
     for step, summed in enumerate(sums, 1):
         route = [(i, (i + 2 * step) % n_head) for i in range(n_head)]
         arrived.append(lax.ppermute(summed, "head", route))
-    steps = 4 if rows % 64 == 0 else 1
+    steps = 2 if rows % 32 == 0 else 1
     row_block = pl.BlockSpec((rows // steps, model), lambda i: (i, 0))
     return pl.pallas_call(
         functools.partial(last_sum, len(near_parts), rows // steps),

time: 175 us -> 178 us (1.017)
  waiting for transfers between devices: 2.56 us -> 5.83 us
    ppermute x3, waiting for transfers between devices: 0.01 us -> 3.28 us  [local(): lax.ppermute(named, 'ctx', [(i, i - 2 * d) for i in range(2 * d, n_ctx)])]
  transfers between devices with their start and end apart: 15 -> 15, of which waited for: 2 -> 5; matrix products, arithmetic and copies ran while one was open for 1% -> 1% of each run, Pallas kernels for 65% -> 64%
where the time goes in v1:
time: 178 us
  Pallas kernels  143 us (80%)
  starting transfers between devices  24 us (13%)
  waiting for transfers between devices  5.83 us (3%)
  local copies, waits for them, and re-layouts  3.26 us (2%)
    pallas_call x3, Pallas kernels, chosen_and_project(): pl.pallas_call(functools.partial(chosen_kernel, heads, (first_chunk, widt...  90.1 us
    pallas_call x2, Pallas kernels, near_branch(): pl.pallas_call(functools.partial(near_kernel, heads, first_block, rims is...  44.7 us
    ppermute x6, starting transfers between devices, all_ahead(): moved.append(lax.ppermute(send, 'ctx', route))  9.91 us
    ppermute x1, starting transfers between devices, local(): lax.ppermute(rim, 'ctx', [(i, i + 1) for i in range(1, n_ctx - 1, 2)])  5.6 us
    pallas_call x3, Pallas kernels, single_step(): pl.pallas_call(kernel, grid_spec=pltpu.PrefetchScalarGridSpec(num_scalar_...  3.99 us
    ppermute x3, starting transfers between devices, local(): lax.ppermute(named, 'ctx', [(i, i - 2 * d) for i in range(2 * d, n_ctx)])  3.88 us
  transfers between devices with their start and end apart: 15, of which 5 were waited for; matrix products, arithmetic and copies ran while one was open for 1% of the time, Pallas kernels for 64%

profile of v1, /device:TPU:5, one launch (start us, length us, event | category | flops | bytes accessed | tf_op | source)
XLA Modules:
  0.0 177.9 jit_solution(2380619947164198940)
XLA Ops:
  0.0 0.9 pad_maximum_fusion.fold_in
  1.0 0.7 copy-done
  1.7 3.2 %prep.1 = (bf16[2656,128]{1,0:T(8,128)(2,1)S(1)}, bf16[1280,128]{1,0:T(8,128)(2,1)}, s32[1,32]{1,0:T(1,128)S(1)}, s32[4,32]{1,0:T(4,128)S(1)}, s32[4,32]{1,0:T(4...) custom-call(s32[7]{0:T(128)S(1)} %stack.31.where_ref.refs_0_, ...), custom_call_target="tpu_custom_call" | custom-call | tf_op jit(solution)/shard_map/prep/pallas_call | solution.py:699
  5.0 1.3 collective-permute-start.2
  6.3 1.3 collective-permute-start.1
  7.6 1.3 collective-permute-start
  8.9 2.2 %collective-permute-done.2.refs_2_.refs_3_ = s32[1,32]{1,0:T(1,128)S(1)} collective-permute-done((s32[1,32]{1,0:T(1,128)S(1)}, s32[1,32]{1,0:T(1,128)S(1)}, u32[]{:S(2)}, u32[]{:S(2)}) %collective-permute-start.2) | collective-permute-done | bytes 160 | tf_op jit(solution)/shard_map/ppermute | solution.py:723
  11.5 0.7 collective-permute-done.refs_0_.refs_1_
  12.2 5.6 %collective-permute-start.4 = (bf16[1280,128]{1,0:T(8,128)(2,1)}, bf16[1280,128]{1,0:T(8,128)(2,1)}, u32[]{:S(2)}, u32[]{:S(2)}) collective-permute-start(bf16[1280,128]{1,0:T(8,128)(2,1)} %get-tuple-element.59), channel_id=1, source_target_pairs={{4,8},{12,16},{20,24},{5,9},{13,17},{21,25},{6,10},{14,18},{22,26}... | collective-permute-start | bytes 983048 | tf_op jit(solution)/shard_map/ppermute | solution.py:749
  17.8 1.3 pack.2
  19.1 0.7 copy-done.1
  19.8 0.7 copy-done.2
  20.4 2.0 %collective-permute-start.5 = (bf16[736,128]{1,0:T(8,128)(2,1)}, bf16[736,128]{1,0:T(8,128)(2,1)}, u32[]{:S(2)}, u32[]{:S(2)}) collective-permute-start(bf16[736,128]{1,0:T(8,128)(2,1)} %get-tuple-element.63), channel_id=1, source_target_pairs={{0,24},{4,28},{1,25},{5,29},{2,26},{6,30},{3,27},{7,31}} | collective-permute-start | bytes 565256 | tf_op jit(solution)/shard_map/ppermute | solution.py:745
  22.4 1.1 copy.13.gate_ref.refs_4_
  23.5 2.0 %collective-permute-start.7 = (bf16[736,128]{1,0:T(8,128)(2,1)}, bf16[736,128]{1,0:T(8,128)(2,1)S(1)}, u32[]{:S(2)}, u32[]{:S(2)}) collective-permute-start(bf16[736,128]{1,0:T(8,128)(2,1)} %copy-done.2), channel_id=1, source_target_pairs={{0,16},{4,20},{8,24},{12,28},{1,17},{5,21},{9,25},{13,29},{2,18},{... | collective-permute-start | bytes 565256 | tf_op jit(solution)/shard_map/ppermute | solution.py:745
  25.5 2.1 %collective-permute-start.9 = (bf16[736,128]{1,0:T(8,128)(2,1)}, bf16[736,128]{1,0:T(8,128)(2,1)S(1)}, u32[]{:S(2)}, u32[]{:S(2)}) collective-permute-start(bf16[736,128]{1,0:T(8,128)(2,1)} %copy-done.1), channel_id=1, source_target_pairs={{0,8},{4,12},{8,16},{12,20},{16,24},{20,28},{1,9},{5,13},{9,17},{1... | collective-permute-start | bytes 565256 | tf_op jit(solution)/shard_map/ppermute | solution.py:745
  27.6 25.9 %near_branch.2.refs_5_ = bf16[1024,2048]{1,0:T(8,128)(2,1)} custom-call(s32[7]{0:T(128)S(1)} %stack.31.where_ref.refs_0_, bf16[1024,3072]{1,0:T(8,128)(2,1)} %refs_3_.5, f32[1024,48]{1,0:T(8,128)S(1)} %copy.13.gate_ref.refs_4_, bf16[256,1024]{1,0:T(8,128)(2,1)S(1)} %get-tuple-element.55.refs_0_, bf16[256,1024]{1,0:T(8,128)(2,1)S(1)} %get-tuple-element.56.refs_1_, ...), custom_call_target="tpu_custom_call" | custom-call | flops 402653184 | bytes 7340032 | tf_op jit(solution)/shard_map/near_branch/pallas_call | solution.py:476
  53.5 0.6 pack.3
  54.2 1.3 collective-permute-start.6
  55.5 1.3 collective-permute-start.8
  56.8 1.3 collective-permute-start.10
  58.1 18.8 %near_branch.3.refs_5_ = bf16[1024,2048]{1,0:T(8,128)(2,1)} custom-call(s32[7]{0:T(128)S(1)} %stack.31.where_ref.refs_0_, bf16[1024,3072]{1,0:T(8,128)(2,1)} %refs_3_.5, f32[1024,48]{1,0:T(8,128)S(1)} %copy.13.gate_ref.refs_4_, bf16[256,1024]{1,0:T(8,128)(2,1)S(1)} %get-tuple-element.55.refs_0_, ...), custom_call_target="tpu_custom_call", output_to_operand_aliasing={{}: (8, {})} | custom-call | flops 402653184 | bytes 7340032 | tf_op jit(solution)/shard_map/near_branch/pallas_call | solution.py:476
  76.9 2.1 %pool.1 = (bf16[2048,256]{1,0:T(8,128)(2,1)S(1)}, bf16[2048,128]{1,0:T(8,128)(2,1)S(1)}, bf16[256,256]{1,0:T(8,128)(2,1)S(1)}, bf16[256,256]{1,0:T(8,128)(2,1)S(1)}, bf16[256,256]{1,0:T(8,128)(2,1)S(1)}) custom-call(s32[7]{0:T(128)S(1)} %stack.31.where_ref.refs_0_, bf16[2656,128]{1,0:T(8,128)(2,1)S(1)} %get-tuple-element.50.refs_3_.own_ref, ...), custom_call_target="tpu_custom_call" | custom-call | tf_op jit(solution)/shard_map/pool/pallas_call | solution.py:635
  79.0 22.9 %chosen_and_project.4 = bf16[256,2560]{1,0:T(8,128)(2,1)S(1)} custom-call(s32[7]{0:T(128)S(1)} %stack.31.where_ref.refs_0_, s32[4,32]{1,0:T(4,128)S(1)} %get-tuple-element.42.refs_1_, s32[4,32]{1,0:T(4,128)S(1)} %get-tuple-element.43.refs_2_, bf16[1024,3072]{1,0:T(8,128)(2,1)} %refs_3_.5, f32[1024,48]{1,0:T(8,128)S(1)} %copy.13.gate_ref.refs_4_, ...), custom_call_target="tpu_custom_call" | custom-call | flops 268435456 | bytes 5242880 | tf_op jit(solution)/shard_map/chosen_and_project/pallas_call | solution.py:595
  101.9 2.7 %collective-permute-start.11 = (bf16[256,2560]{1,0:T(8,128)(2,1)S(1)}, bf16[256,2560]{1,0:T(8,128)(2,1)S(1)}, u32[]{:S(2)}, u32[]{:S(2)}) collective-permute-start(bf16[256,2560]{1,0:T(8,128)(2,1)S(1)} %chosen_and_project.4), channel_id=1, source_target_pairs={{0,1},{1,0},{2,3},{3,2},{4,5},{5,4},{6,7},{7,6},{8,9},{9,8},{10,11... | collective-permute-start | bytes 3932168 | tf_op jit(solution)/shard_map/ppermute | solution.py:790
  104.6 23.1 %chosen_and_project.3 = bf16[256,2560]{1,0:T(8,128)(2,1)S(1)} custom-call(s32[7]{0:T(128)S(1)} %stack.31.where_ref.refs_0_, s32[4,32]{1,0:T(4,128)S(1)} %get-tuple-element.42.refs_1_, s32[4,32]{1,0:T(4,128)S(1)} %get-tuple-element.43.refs_2_, bf16[1024,3072]{1,0:T(8,128)(2,1)} %refs_3_.5, f32[1024,48]{1,0:T(8,128)S(1)} %copy.13.gate_ref.refs_4_, ...), custom_call_target="tpu_custom_call" | custom-call | flops 268435456 | bytes 5242880 | tf_op jit(solution)/shard_map/chosen_and_project/pallas_call | solution.py:595
  128.0 1.3 collective-permute-start.14
  129.3 44.2 %chosen_and_project.5 = (bf16[256,1280]{1,0:T(8,128)(2,1)S(1)}, bf16[256,1280]{1,0:T(8,128)(2,1)S(1)}, bf16[256,2560]{1,0:T(8,128)(2,1)S(1)}) custom-call(s32[7]{0:T(128)S(1)} %stack.31.where_ref.refs_0_, s32[4,32]{1,0:T(4,128)S(1)} %get-tuple-element.42.refs_1_, s32[4,32]{1,0:T(4,128)S(1)} %get-tuple-element.43.refs_2_, bf16[1024,3072]{1,0:T(8,128)(2,1)} %refs_3_.5, ...), custom_call_target="tpu_custom_call" | custom-call | flops 268435456 | bytes 5242880 | tf_op jit(solution)/shard_map/chosen_and_project/pallas_call | solution.py:595
  173.6 0.5 collective-permute-start.13
  174.0 1.6 collective-permute-done.12.refs_0_
  175.6 0.9 collective-permute-done.13.refs_1_
  176.6 1.3 last_sum.1
  (18 shorter events, 1.0 us)
Async XLA Ops:
  1.0 0.7 copy-start
  4.9 48.6 %collective-permute-start.3 = (bf16[2656,128]{1,0:T(8,128)(2,1)S(1)}, bf16[2656,128]{1,0:T(8,128)(2,1)S(1)}, u32[]{:S(2)}, u32[]{:S(2)}) collective-permute-start(bf16[2656,128]{1,0:T(8,128)(2,1)S(1)} %get-tuple-element.50.refs_3_.own_ref), channel_id=1, source_target_pairs={{0,4},{4,0},{8,12},{12,8},{16,20},{20,16},{24,28},{28,24},{1,5},{5... | collective-permute-start | bytes 2039816 | tf_op jit(solution)/shard_map/ppermute | solution.py:721
  5.0 6.1 %collective-permute-start.2 = (s32[1,32]{1,0:T(1,128)S(1)}, s32[1,32]{1,0:T(1,128)S(1)}, u32[]{:S(2)}, u32[]{:S(2)}) collective-permute-start(s32[1,32]{1,0:T(1,128)S(1)} %get-tuple-element.61.refs_0_), channel_id=1, source_target_pairs={{24,0},{28,4},{25,1},{29,5},{26,2},{30,6},{27,3},{31,7}} | collective-permute-start | bytes 392 | tf_op jit(solution)/shard_map/ppermute | solution.py:723
  6.3 5.2 %collective-permute-start.1 = (s32[1,32]{1,0:T(1,128)S(1)}, s32[1,32]{1,0:T(1,128)S(1)}, u32[]{:S(2)}, u32[]{:S(2)}) collective-permute-start(s32[1,32]{1,0:T(1,128)S(1)} %get-tuple-element.61.refs_0_), channel_id=1, source_target_pairs={{16,0},{20,4},{24,8},{28,12},{17,1},{21,5},{25,9},{29,13},{18,2},{... | collective-permute-start | bytes 392 | tf_op jit(solution)/shard_map/ppermute | solution.py:723
  7.6 4.6 %collective-permute-start = (s32[1,32]{1,0:T(1,128)S(1)}, s32[1,32]{1,0:T(1,128)S(1)}, u32[]{:S(2)}, u32[]{:S(2)}) collective-permute-start(s32[1,32]{1,0:T(1,128)S(1)} %get-tuple-element.61.refs_0_), channel_id=1, source_target_pairs={{8,0},{12,4},{16,8},{20,12},{24,16},{28,20},{9,1},{13,5},{17,9},{2... | collective-permute-start | bytes 392 | tf_op jit(solution)/shard_map/ppermute | solution.py:723
  12.2 44.6 %collective-permute-start.4 = (bf16[1280,128]{1,0:T(8,128)(2,1)}, bf16[1280,128]{1,0:T(8,128)(2,1)}, u32[]{:S(2)}, u32[]{:S(2)}) collective-permute-start(bf16[1280,128]{1,0:T(8,128)(2,1)} %get-tuple-element.59), channel_id=1, source_target_pairs={{4,8},{12,16},{20,24},{5,9},{13,17},{21,25},{6,10},{14,18},{22,26}... | collective-permute-start | bytes 983048 | tf_op jit(solution)/shard_map/ppermute | solution.py:749
  19.1 0.7 copy-start.1
  19.8 0.7 copy-start.2
  20.4 35.0 %collective-permute-start.5 = (bf16[736,128]{1,0:T(8,128)(2,1)}, bf16[736,128]{1,0:T(8,128)(2,1)}, u32[]{:S(2)}, u32[]{:S(2)}) collective-permute-start(bf16[736,128]{1,0:T(8,128)(2,1)} %get-tuple-element.63), channel_id=1, source_target_pairs={{0,24},{4,28},{1,25},{5,29},{2,26},{6,30},{3,27},{7,31}} | collective-permute-start | bytes 565256 | tf_op jit(solution)/shard_map/ppermute | solution.py:745
  23.5 53.4 %collective-permute-start.7 = (bf16[736,128]{1,0:T(8,128)(2,1)}, bf16[736,128]{1,0:T(8,128)(2,1)S(1)}, u32[]{:S(2)}, u32[]{:S(2)}) collective-permute-start(bf16[736,128]{1,0:T(8,128)(2,1)} %copy-done.2), channel_id=1, source_target_pairs={{0,16},{4,20},{8,24},{12,28},{1,17},{5,21},{9,25},{13,29},{2,18},{... | collective-permute-start | bytes 565256 | tf_op jit(solution)/shard_map/ppermute | solution.py:745
  25.5 51.4 %collective-permute-start.9 = (bf16[736,128]{1,0:T(8,128)(2,1)}, bf16[736,128]{1,0:T(8,128)(2,1)S(1)}, u32[]{:S(2)}, u32[]{:S(2)}) collective-permute-start(bf16[736,128]{1,0:T(8,128)(2,1)} %copy-done.1), channel_id=1, source_target_pairs={{0,8},{4,12},{8,16},{12,20},{16,24},{20,28},{1,9},{5,13},{9,17},{1... | collective-permute-start | bytes 565256 | tf_op jit(solution)/shard_map/ppermute | solution.py:745
  54.2 22.7 %collective-permute-start.6 = (bf16[736,128]{1,0:T(8,128)(2,1)S(1)}, bf16[736,128]{1,0:T(8,128)(2,1)S(1)}, u32[]{:S(2)}, u32[]{:S(2)}) collective-permute-start(bf16[736,128]{1,0:T(8,128)(2,1)S(1)} %get-tuple-element.64), channel_id=1, source_target_pairs={{0,24},{4,28},{1,25},{5,29},{2,26},{6,30},{3,27},{7,31}} | collective-permute-start | bytes 565256 | tf_op jit(solution)/shard_map/ppermute | solution.py:745
  55.5 21.4 %collective-permute-start.8 = (bf16[736,128]{1,0:T(8,128)(2,1)S(1)}, bf16[736,128]{1,0:T(8,128)(2,1)S(1)}, u32[]{:S(2)}, u32[]{:S(2)}) collective-permute-start(bf16[736,128]{1,0:T(8,128)(2,1)S(1)} %get-tuple-element.66), channel_id=1, source_target_pairs={{0,16},{4,20},{8,24},{12,28},{1,17},{5,21},{9,25},{13,29},{2,18},{... | collective-permute-start | bytes 565256 | tf_op jit(solution)/shard_map/ppermute | solution.py:745
  56.8 20.1 %collective-permute-start.10 = (bf16[736,128]{1,0:T(8,128)(2,1)S(1)}, bf16[736,128]{1,0:T(8,128)(2,1)S(1)}, u32[]{:S(2)}, u32[]{:S(2)}) collective-permute-start(bf16[736,128]{1,0:T(8,128)(2,1)S(1)} %get-tuple-element.68), channel_id=1, source_target_pairs={{0,8},{4,12},{8,16},{12,20},{16,24},{20,28},{1,9},{5,13},{9,17},{1... | collective-permute-start | bytes 565256 | tf_op jit(solution)/shard_map/ppermute | solution.py:745
  101.9 25.8 %collective-permute-start.11 = (bf16[256,2560]{1,0:T(8,128)(2,1)S(1)}, bf16[256,2560]{1,0:T(8,128)(2,1)S(1)}, u32[]{:S(2)}, u32[]{:S(2)}) collective-permute-start(bf16[256,2560]{1,0:T(8,128)(2,1)S(1)} %chosen_and_project.4), channel_id=1, source_target_pairs={{0,1},{1,0},{2,3},{3,2},{4,5},{5,4},{6,7},{7,6},{8,9},{9,8},{10,11... | collective-permute-start | bytes 3932168 | tf_op jit(solution)/shard_map/ppermute | solution.py:790
  128.0 48.6 %collective-permute-start.14 = (bf16[256,2560]{1,0:T(8,128)(2,1)S(1)}, bf16[256,2560]{1,0:T(8,128)(2,1)S(1)}, u32[]{:S(2)}, u32[]{:S(2)}) collective-permute-start(bf16[256,2560]{1,0:T(8,128)(2,1)S(1)} %add_convert_fusion), channel_id=1, source_target_pairs={{0,2},{1,3},{2,0},{3,1},{4,6},{5,7},{6,4},{7,5},{8,10},{9,11},{10,... | collective-permute-start | bytes 3932168 | tf_op jit(solution)/shard_map/ppermute | solution.py:800
  173.5 2.2 %collective-permute-start.12 = (bf16[256,1280]{1,0:T(8,128)(2,1)S(1)}, bf16[256,1280]{1,0:T(8,128)(2,1)S(1)}, u32[]{:S(2)}, u32[]{:S(2)}) collective-permute-start(bf16[256,1280]{1,0:T(8,128)(2,1)S(1)} %get-tuple-element.76), channel_id=1, source_target_pairs={{0,1},{1,0},{2,3},{3,2},{4,5},{5,4},{6,7},{7,6},{8,9},{9,8},{10,11... | collective-permute-start | bytes 1966088 | tf_op jit(solution)/shard_map/ppermute | solution.py:796
  173.6 3.0 %collective-permute-start.13 = (bf16[256,1280]{1,0:T(8,128)(2,1)S(1)}, bf16[256,1280]{1,0:T(8,128)(2,1)S(1)}, u32[]{:S(2)}, u32[]{:S(2)}) collective-permute-start(bf16[256,1280]{1,0:T(8,128)(2,1)S(1)} %get-tuple-element.77), channel_id=1, source_target_pairs={{0,1},{1,0},{2,3},{3,2},{4,5},{5,4},{6,7},{7,6},{8,9},{9,8},{10,11... | collective-permute-start | bytes 1966088 | tf_op jit(solution)/shard_map/ppermute | solution.py:796

commit v2 on v0

--- a/solution.py
+++ b/solution.py
@@ -184,12 +184,15 @@
     folds = rows // CBLK
 
     def fold(x, w):
-        return jnp.sum(x.reshape(folds, CBLK, 128) * w[None], axis=1).astype(BF16)
+        return jnp.sum(x.reshape(folds, CBLK, 128) * w[None], axis=1)
 
     at = count * BROWS
-    packed_ref[at : at + folds] = fold(low, wlow)
-    packed_ref[at + folds : at + 2 * folds] = fold(high, whigh)
-    packed_ref[at + 2 * folds :] = fold(values.astype(F32), vw_ref[...])
+    half = folds // 2
+    high_fold = fold(high, whigh)
+    high_fold = high_fold[:half] + swap_halves(high_fold[half:])
+    packed_ref[at : at + folds] = fold(low, wlow).astype(BF16)
+    packed_ref[at + folds : at + folds + half] = high_fold.astype(BF16)
+    packed_ref[at + folds + half :] = fold(values.astype(F32), vw_ref[...]).astype(BF16)
 
 
 def pack_kernel(lists, beside, where_ref, *refs):
@@ -258,7 +261,8 @@
     parity = lax.rem(shard, 2)
     base = shard - parity
     rows = lists * KBLK
-    folds = (ins[0].shape[0] - lists * BROWS) // 3
+    folds = (ins[0].shape[0] - lists * BROWS) * 2 // 5
+    half = folds // 2
     folded[...] = jnp.zeros_like(folded)
     cval_ref[...] = jnp.zeros_like(cval_ref)
 
@@ -268,12 +272,15 @@
         key_ref[at] = keys
         val_ref[at] = values
         low = ref[fold_at : fold_at + folds]
-        high = ref[fold_at + folds : fold_at + 2 * folds]
+        high = ref[fold_at + folds : fold_at + folds + half].astype(F32)
+        left = half_lanes(half)
+        high = [jnp.where(left, x, 0.0) for x in (high, swap_halves(high))]
+        high = jnp.concatenate(high, axis=0).astype(BF16)
         owned = pl.ds(pl.multiple_of(owner * folds, 32), folds)
         folded[owned] = jnp.concatenate([low, high], axis=1)
-        cval_ref[owned] = with_ones(ref[fold_at + 2 * folds : fold_at + 3 * folds])
-
-    fill(0, shard, own_ref, QBLK // KBLK, own_ref.shape[0] - 3 * folds)
+        cval_ref[owned] = with_ones(ref[fold_at + folds + half : fold_at + 2 * folds + half])
+
+    fill(0, shard, own_ref, QBLK // KBLK, own_ref.shape[0] - 2 * folds - half)
     fill(1, base + 1 - parity, ins[0], 1, lists * BROWS)
     for distance in range(1, groups):
 
@@ -660,7 +667,7 @@
     rim_rows = rim_blocks * BROWS
     fold_weights = jnp.concatenate([comp_key_weight, comp_value_weight], axis=1)
     int32 = lambda *shape: jax.ShapeDtypeStruct(shape, jnp.int32)
-    prep_out = [bf16(packed_rows + 3 * folds, 128), bf16(rim_rows, 128)]
+    prep_out = [bf16(packed_rows + folds * 5 // 2, 128), bf16(rim_rows, 128)]
     prep_out += [int32(1, n_ctx * lists), int32(lists, 2 * PICKS), int32(lists, 2 * PICKS)]
     prep_out += [bf16(256, tokens)] * 2 + [bf16(tokens, 256)]
     packed, rim, named, slots, dead, even, odd, val = pl.pallas_call(
@@ -694,7 +701,7 @@
 
     gates = jax.nn.sigmoid(gate_logits).reshape(tokens, 3 * heads)
     gates = jnp.pad(gates, ((0, 0), (0, 128 - 3 * heads)))
-    sent = bf16(lists * BROWS + 3 * folds, 128)
+    sent = bf16(lists * BROWS + folds * 5 // 2, 128)
 
     def pack(beside, lists_in, rows):
         return single_step(
@@ -766,7 +773,7 @@
     for step, summed in enumerate(sums, 1):
         route = [(i, (i + 2 * step) % n_head) for i in range(n_head)]
         arrived.append(lax.ppermute(summed, "head", route))
-    steps = 4 if rows % 64 == 0 else 1
+    steps = 2 if rows % 32 == 0 else 1
     row_block = pl.BlockSpec((rows // steps, model), lambda i: (i, 0))
     return pl.pallas_call(
         functools.partial(last_sum, len(near_parts), rows // steps),

time: 175 us -> 174 us (level)
  no operation moved by 1% of the time
where the time goes in v2:
time: 174 us; the launch traced here: 173 us
  Pallas kernels  142 us (82%)
  starting transfers between devices  24.4 us (14%)
  local copies, waits for them, and re-layouts  2.87 us (2%)
  waiting for transfers between devices  2.56 us (1%)
    pallas_call x3, Pallas kernels, chosen_and_project(): pl.pallas_call(functools.partial(chosen_kernel, heads, (first_chunk, widt...  90.5 us
    pallas_call x2, Pallas kernels, near_branch(): pl.pallas_call(functools.partial(near_kernel, heads, first_block, rims is...  44.2 us
    ppermute x6, starting transfers between devices, all_ahead(): moved.append(lax.ppermute(send, 'ctx', route))  11 us
    ppermute x1, starting transfers between devices, local(): lax.ppermute(rim, 'ctx', [(i, i + 1) for i in range(1, n_ctx - 1, 2)])  5.16 us
    ppermute x3, starting transfers between devices, local(): lax.ppermute(named, 'ctx', [(i, i - 2 * d) for i in range(2 * d, n_ctx)])  3.88 us
  transfers between devices with their start and end apart: 15, of which 2 were waited for; matrix products, arithmetic and copies ran while one was open for 1% of the time, Pallas kernels for 65%

profile of v2, /device:TPU:5, one launch (start us, length us, event | category | flops | bytes accessed | tf_op | source)
XLA Modules:
  0.0 173.0 jit_solution(9932731680119462360)
XLA Ops:
  0.0 0.9 pad_maximum_fusion.fold_in
  0.9 0.1 stack.31.where_ref.refs_0_
  1.0 0.7 copy-done
  1.7 3.2 %prep.1 = (bf16[2640,128]{1,0:T(8,128)(2,1)S(1)}, bf16[1280,128]{1,0:T(8,128)(2,1)}, s32[1,32]{1,0:T(1,128)S(1)}, s32[4,32]{1,0:T(4,128)S(1)}, s32[4,32]{1,0:T(4...) custom-call(s32[7]{0:T(128)S(1)} %stack.31.where_ref.refs_0_, ...), custom_call_target="tpu_custom_call" | custom-call | tf_op jit(solution)/shard_map/prep/pallas_call | solution.py:673
  5.0 1.3 collective-permute-start.2
  6.3 1.3 collective-permute-start.1
  7.6 1.3 collective-permute-start
  8.9 5.2 %collective-permute-start.4 = (bf16[1280,128]{1,0:T(8,128)(2,1)}, bf16[1280,128]{1,0:T(8,128)(2,1)S(1)}, u32[]{:S(2)}, u32[]{:S(2)}) collective-permute-start(bf16[1280,128]{1,0:T(8,128)(2,1)} %get-tuple-element.57), channel_id=1, source_target_pairs={{4,8},{12,16},{20,24},{5,9},{13,17},{21,25},{6,10},{14,18},{22,26}... | collective-permute-start | bytes 983048 | tf_op jit(solution)/shard_map/ppermute | solution.py:700
  14.2 1.0 copy.11
  15.2 1.1 pad.4.gate_ref.refs_4_
  16.3 0.6 pack.2
  16.9 2.2 %collective-permute-start.5 = (bf16[720,128]{1,0:T(8,128)(2,1)S(1)}, bf16[720,128]{1,0:T(8,128)(2,1)S(1)}, u32[]{:S(2)}, u32[]{:S(2)}) collective-permute-start(bf16[720,128]{1,0:T(8,128)(2,1)S(1)} %get-tuple-element.61), channel_id=1, source_target_pairs={{0,24},{4,28},{1,25},{5,29},{2,26},{6,30},{3,27},{7,31}} | collective-permute-start | bytes 552968 | tf_op jit(solution)/shard_map/ppermute | solution.py:721
  19.1 3.4 %collective-permute-start.7 = (bf16[720,128]{1,0:T(8,128)(2,1)S(1)}, bf16[720,128]{1,0:T(8,128)(2,1)S(1)}, u32[]{:S(2)}, u32[]{:S(2)}) collective-permute-start(bf16[720,128]{1,0:T(8,128)(2,1)S(1)} %get-tuple-element.63), channel_id=1, source_target_pairs={{0,16},{4,20},{8,24},{12,28},{1,17},{5,21},{9,25},{13,29},{2,18},{... | collective-permute-start | bytes 552968 | tf_op jit(solution)/shard_map/ppermute | solution.py:721
  22.5 1.3 collective-permute-start.9
  23.8 25.6 %near_branch.2.refs_5_ = bf16[1024,2048]{1,0:T(8,128)(2,1)} custom-call(s32[7]{0:T(128)S(1)} %stack.31.where_ref.refs_0_, bf16[1024,3072]{1,0:T(8,128)(2,1)} %refs_3_.5, f32[1024,128]{1,0:T(8,128)S(1)} %pad.4.gate_ref.refs_4_, bf16[256,1024]{1,0:T(8,128)(2,1)S(1)} %get-tuple-element.53.refs_0_, bf16[256,1024]{1,0:T(8,128)(2,1)S(1)} %get-tuple-element.54.refs_1_, ...), custom_call_target="tpu_custom_call" | custom-call | flops 402653184 | bytes 7340032 | tf_op jit(solution)/shard_map/near_branch/pallas_call | solution.py:451
  49.4 0.6 pack.3
  50.0 1.3 collective-permute-start.6
  51.3 1.3 collective-permute-start.8
  52.6 1.5 collective-permute-start.10
  54.2 18.6 %near_branch.3.refs_5_ = bf16[1024,2048]{1,0:T(8,128)(2,1)} custom-call(s32[7]{0:T(128)S(1)} %stack.31.where_ref.refs_0_, bf16[1024,3072]{1,0:T(8,128)(2,1)} %refs_3_.5, f32[1024,128]{1,0:T(8,128)S(1)} %pad.4.gate_ref.refs_4_, bf16[256,1024]{1,0:T(8,128)(2,1)S(1)} %get-tuple-element.53.refs_0_, ...), custom_call_target="tpu_custom_call", output_to_operand_aliasing={{}: (8, {})} | custom-call | flops 402653184 | bytes 7340032 | tf_op jit(solution)/shard_map/near_branch/pallas_call | solution.py:451
  72.9 1.1 pool.1
  74.0 23.0 %chosen_and_project.4 = bf16[256,2560]{1,0:T(8,128)(2,1)S(1)} custom-call(s32[7]{0:T(128)S(1)} %stack.31.where_ref.refs_0_, s32[4,32]{1,0:T(4,128)S(1)} %get-tuple-element.41.refs_1_, s32[4,32]{1,0:T(4,128)S(1)} %get-tuple-element.42.refs_2_, bf16[1024,3072]{1,0:T(8,128)(2,1)} %refs_3_.5, f32[1024,128]{1,0:T(8,128)S(1)} %pad.4.gate_ref.refs_4_, ...), custom_call_target="tpu_custom_call" | custom-call | flops 268435456 | bytes 5242880 | tf_op jit(solution)/shard_map/chosen_and_project/pallas_call | solution.py:570
  97.0 2.4 %collective-permute-start.11 = (bf16[256,2560]{1,0:T(8,128)(2,1)S(1)}, bf16[256,2560]{1,0:T(8,128)(2,1)S(1)}, u32[]{:S(2)}, u32[]{:S(2)}) collective-permute-start(bf16[256,2560]{1,0:T(8,128)(2,1)S(1)} %chosen_and_project.4), channel_id=1, source_target_pairs={{0,1},{1,0},{2,3},{3,2},{4,5},{5,4},{6,7},{7,6},{8,9},{9,8},{10,11... | collective-permute-start | bytes 3932168 | tf_op jit(solution)/shard_map/ppermute | solution.py:765
  99.4 23.2 %chosen_and_project.3 = bf16[256,2560]{1,0:T(8,128)(2,1)S(1)} custom-call(s32[7]{0:T(128)S(1)} %stack.31.where_ref.refs_0_, s32[4,32]{1,0:T(4,128)S(1)} %get-tuple-element.41.refs_1_, s32[4,32]{1,0:T(4,128)S(1)} %get-tuple-element.42.refs_2_, bf16[1024,3072]{1,0:T(8,128)(2,1)} %refs_3_.5, f32[1024,128]{1,0:T(8,128)S(1)} %pad.4.gate_ref.refs_4_, ...), custom_call_target="tpu_custom_call" | custom-call | flops 268435456 | bytes 5242880 | tf_op jit(solution)/shard_map/chosen_and_project/pallas_call | solution.py:570
  122.6 0.3 add_convert_fusion
  122.9 1.3 collective-permute-start.14
  124.2 44.3 %chosen_and_project.5 = (bf16[256,1280]{1,0:T(8,128)(2,1)S(1)}, bf16[256,1280]{1,0:T(8,128)(2,1)S(1)}, bf16[256,2560]{1,0:T(8,128)(2,1)S(1)}) custom-call(s32[7]{0:T(128)S(1)} %stack.31.where_ref.refs_0_, s32[4,32]{1,0:T(4,128)S(1)} %get-tuple-element.41.refs_1_, s32[4,32]{1,0:T(4,128)S(1)} %get-tuple-element.42.refs_2_, bf16[1024,3072]{1,0:T(8,128)(2,1)} %refs_3_.5, ...), custom_call_target="tpu_custom_call" | custom-call | flops 268435456 | bytes 5242880 | tf_op jit(solution)/shard_map/chosen_and_project/pallas_call | solution.py:570
  168.6 0.4 collective-permute-start.12
  168.9 0.2 collective-permute-start.13
  169.1 1.6 collective-permute-done.12.refs_0_
  170.7 0.9 collective-permute-done.13.refs_1_
  171.7 1.3 last_sum.1
  (18 shorter events, 0.2 us)
Async XLA Ops:
  1.0 0.7 copy-start
  1.7 12.4 %copy-start.1 = (f32[1024,3,16]{0,2,1:T(8,128)S(1)}, f32[1024,3,16]{0,2,1:T(8,128)}, u32[]{:S(2)}) copy-start(f32[1024,3,16]{0,2,1:T(8,128)} %param.14) | copy-start | bytes 589828
  4.9 44.4 %collective-permute-start.3 = (bf16[2640,128]{1,0:T(8,128)(2,1)S(1)}, bf16[2640,128]{1,0:T(8,128)(2,1)S(1)}, u32[]{:S(2)}, u32[]{:S(2)}) collective-permute-start(bf16[2640,128]{1,0:T(8,128)(2,1)S(1)} %get-tuple-element.48.refs_3_.own_ref), channel_id=1, source_target_pairs={{0,4},{4,0},{8,12},{12,8},{16,20},{20,16},{24,28},{28,24},{1,5},{5... | collective-permute-start | bytes 2027528 | tf_op jit(solution)/shard_map/ppermute | solution.py:695
  5.0 11.2 %collective-permute-start.2 = (s32[1,32]{1,0:T(1,128)S(1)}, s32[1,32]{1,0:T(1,128)S(1)}, u32[]{:S(2)}, u32[]{:S(2)}) collective-permute-start(s32[1,32]{1,0:T(1,128)S(1)} %get-tuple-element.59.refs_0_), channel_id=1, source_target_pairs={{24,0},{28,4},{25,1},{29,5},{26,2},{30,6},{27,3},{31,7}} | collective-permute-start | bytes 392 | tf_op jit(solution)/shard_map/ppermute | solution.py:697
  6.3 9.9 %collective-permute-start.1 = (s32[1,32]{1,0:T(1,128)S(1)}, s32[1,32]{1,0:T(1,128)S(1)}, u32[]{:S(2)}, u32[]{:S(2)}) collective-permute-start(s32[1,32]{1,0:T(1,128)S(1)} %get-tuple-element.59.refs_0_), channel_id=1, source_target_pairs={{16,0},{20,4},{24,8},{28,12},{17,1},{21,5},{25,9},{29,13},{18,2},{... | collective-permute-start | bytes 392 | tf_op jit(solution)/shard_map/ppermute | solution.py:697
  7.6 8.7 %collective-permute-start = (s32[1,32]{1,0:T(1,128)S(1)}, s32[1,32]{1,0:T(1,128)S(1)}, u32[]{:S(2)}, u32[]{:S(2)}) collective-permute-start(s32[1,32]{1,0:T(1,128)S(1)} %get-tuple-element.59.refs_0_), channel_id=1, source_target_pairs={{8,0},{12,4},{16,8},{20,12},{24,16},{28,20},{9,1},{13,5},{17,9},{2... | collective-permute-start | bytes 392 | tf_op jit(solution)/shard_map/ppermute | solution.py:697
  8.9 43.7 %collective-permute-start.4 = (bf16[1280,128]{1,0:T(8,128)(2,1)}, bf16[1280,128]{1,0:T(8,128)(2,1)S(1)}, u32[]{:S(2)}, u32[]{:S(2)}) collective-permute-start(bf16[1280,128]{1,0:T(8,128)(2,1)} %get-tuple-element.57), channel_id=1, source_target_pairs={{4,8},{12,16},{20,24},{5,9},{13,17},{21,25},{6,10},{14,18},{22,26}... | collective-permute-start | bytes 983048 | tf_op jit(solution)/shard_map/ppermute | solution.py:700
  16.9 34.4 %collective-permute-start.5 = (bf16[720,128]{1,0:T(8,128)(2,1)S(1)}, bf16[720,128]{1,0:T(8,128)(2,1)S(1)}, u32[]{:S(2)}, u32[]{:S(2)}) collective-permute-start(bf16[720,128]{1,0:T(8,128)(2,1)S(1)} %get-tuple-element.61), channel_id=1, source_target_pairs={{0,24},{4,28},{1,25},{5,29},{2,26},{6,30},{3,27},{7,31}} | collective-permute-start | bytes 552968 | tf_op jit(solution)/shard_map/ppermute | solution.py:721
  19.1 53.7 %collective-permute-start.7 = (bf16[720,128]{1,0:T(8,128)(2,1)S(1)}, bf16[720,128]{1,0:T(8,128)(2,1)S(1)}, u32[]{:S(2)}, u32[]{:S(2)}) collective-permute-start(bf16[720,128]{1,0:T(8,128)(2,1)S(1)} %get-tuple-element.63), channel_id=1, source_target_pairs={{0,16},{4,20},{8,24},{12,28},{1,17},{5,21},{9,25},{13,29},{2,18},{... | collective-permute-start | bytes 552968 | tf_op jit(solution)/shard_map/ppermute | solution.py:721
  22.5 50.4 %collective-permute-start.9 = (bf16[720,128]{1,0:T(8,128)(2,1)S(1)}, bf16[720,128]{1,0:T(8,128)(2,1)S(1)}, u32[]{:S(2)}, u32[]{:S(2)}) collective-permute-start(bf16[720,128]{1,0:T(8,128)(2,1)S(1)} %get-tuple-element.65), channel_id=1, source_target_pairs={{0,8},{4,12},{8,16},{12,20},{16,24},{20,28},{1,9},{5,13},{9,17},{1... | collective-permute-start | bytes 552968 | tf_op jit(solution)/shard_map/ppermute | solution.py:721
  50.0 22.8 %collective-permute-start.6 = (bf16[720,128]{1,0:T(8,128)(2,1)S(1)}, bf16[720,128]{1,0:T(8,128)(2,1)S(1)}, u32[]{:S(2)}, u32[]{:S(2)}) collective-permute-start(bf16[720,128]{1,0:T(8,128)(2,1)S(1)} %get-tuple-element.62), channel_id=1, source_target_pairs={{0,24},{4,28},{1,25},{5,29},{2,26},{6,30},{3,27},{7,31}} | collective-permute-start | bytes 552968 | tf_op jit(solution)/shard_map/ppermute | solution.py:721
  51.3 21.5 %collective-permute-start.8 = (bf16[720,128]{1,0:T(8,128)(2,1)S(1)}, bf16[720,128]{1,0:T(8,128)(2,1)S(1)}, u32[]{:S(2)}, u32[]{:S(2)}) collective-permute-start(bf16[720,128]{1,0:T(8,128)(2,1)S(1)} %get-tuple-element.64), channel_id=1, source_target_pairs={{0,16},{4,20},{8,24},{12,28},{1,17},{5,21},{9,25},{13,29},{2,18},{... | collective-permute-start | bytes 552968 | tf_op jit(solution)/shard_map/ppermute | solution.py:721
  52.6 20.2 %collective-permute-start.10 = (bf16[720,128]{1,0:T(8,128)(2,1)S(1)}, bf16[720,128]{1,0:T(8,128)(2,1)S(1)}, u32[]{:S(2)}, u32[]{:S(2)}) collective-permute-start(bf16[720,128]{1,0:T(8,128)(2,1)S(1)} %get-tuple-element.66), channel_id=1, source_target_pairs={{0,8},{4,12},{8,16},{12,20},{16,24},{20,28},{1,9},{5,13},{9,17},{1... | collective-permute-start | bytes 552968 | tf_op jit(solution)/shard_map/ppermute | solution.py:721
  97.0 25.6 %collective-permute-start.11 = (bf16[256,2560]{1,0:T(8,128)(2,1)S(1)}, bf16[256,2560]{1,0:T(8,128)(2,1)S(1)}, u32[]{:S(2)}, u32[]{:S(2)}) collective-permute-start(bf16[256,2560]{1,0:T(8,128)(2,1)S(1)} %chosen_and_project.4), channel_id=1, source_target_pairs={{0,1},{1,0},{2,3},{3,2},{4,5},{5,4},{6,7},{7,6},{8,9},{9,8},{10,11... | collective-permute-start | bytes 3932168 | tf_op jit(solution)/shard_map/ppermute | solution.py:765
  122.9 48.7 %collective-permute-start.14 = (bf16[256,2560]{1,0:T(8,128)(2,1)S(1)}, bf16[256,2560]{1,0:T(8,128)(2,1)S(1)}, u32[]{:S(2)}, u32[]{:S(2)}) collective-permute-start(bf16[256,2560]{1,0:T(8,128)(2,1)S(1)} %add_convert_fusion), channel_id=1, source_target_pairs={{0,2},{1,3},{2,0},{3,1},{4,6},{5,7},{6,4},{7,5},{8,10},{9,11},{10,... | collective-permute-start | bytes 3932168 | tf_op jit(solution)/shard_map/ppermute | solution.py:775
  168.6 2.2 %collective-permute-start.12 = (bf16[256,1280]{1,0:T(8,128)(2,1)S(1)}, bf16[256,1280]{1,0:T(8,128)(2,1)S(1)}, u32[]{:S(2)}, u32[]{:S(2)}) collective-permute-start(bf16[256,1280]{1,0:T(8,128)(2,1)S(1)} %get-tuple-element.74), channel_id=1, source_target_pairs={{0,1},{1,0},{2,3},{3,2},{4,5},{5,4},{6,7},{7,6},{8,9},{9,8},{10,11... | collective-permute-start | bytes 1966088 | tf_op jit(solution)/shard_map/ppermute | solution.py:771
  168.9 2.7 %collective-permute-start.13 = (bf16[256,1280]{1,0:T(8,128)(2,1)S(1)}, bf16[256,1280]{1,0:T(8,128)(2,1)S(1)}, u32[]{:S(2)}, u32[]{:S(2)}) collective-permute-start(bf16[256,1280]{1,0:T(8,128)(2,1)S(1)} %get-tuple-element.75), channel_id=1, source_target_pairs={{0,1},{1,0},{2,3},{3,2},{4,5},{5,4},{6,7},{7,6},{8,9},{9,8},{10,11... | collective-permute-start | bytes 1966088 | tf_op jit(solution)/shard_map/ppermute | solution.py:771

commit v3 on v2

--- a/solution.py
+++ b/solution.py
@@ -697,7 +697,6 @@
         lax.ppermute(named, "ctx", [(i, i - 2 * d) for i in range(2 * d, n_ctx)])
         for d in range(1, groups)
     ]
-    far_rim = lax.ppermute(rim, "ctx", [(i, i + 1) for i in range(1, n_ctx - 1, 2)])
 
     gates = jax.nn.sigmoid(gate_logits).reshape(tokens, 3 * heads)
     gates = jnp.pad(gates, ((0, 0), (0, 128 - 3 * heads)))
@@ -723,8 +722,9 @@
 
     named, gates = lax.optimization_barrier((named, gates))
     own_sends = pack(False, named[1:], packed)
-    own_sends, even = lax.optimization_barrier((own_sends, even))
+    own_sends, even, rim = lax.optimization_barrier((own_sends, even, rim))
     from_same = all_ahead(own_sends)
+    far_rim = lax.ppermute(rim, "ctx", [(i, i + 1) for i in range(1, n_ctx - 1, 2)])
 
     reach = WINDOW // QBLK
     near = functools.partial(near_branch, where=where, queries=queries, gates=gates)

time: 174 us -> 173 us (level)
  transfers between devices with their start and end apart: 15 -> 15, of which waited for: 2 -> 4; matrix products, arithmetic and copies ran while one was open for 1% -> 1% of each run, Pallas kernels for 65% -> 65%
where the time goes in v3:
time: 173 us; the launch traced here: 172 us
  Pallas kernels  141 us (82%)
  starting transfers between devices  23.3 us (13%)
  waiting for transfers between devices  3.67 us (2%)
  local copies, waits for them, and re-layouts  2.87 us (2%)
    pallas_call x3, Pallas kernels, chosen_and_project(): pl.pallas_call(functools.partial(chosen_kernel, heads, (first_chunk, widt...  90.3 us
    pallas_call x2, Pallas kernels, near_branch(): pl.pallas_call(functools.partial(near_kernel, heads, first_block, rims is...  44.2 us
    ppermute x6, starting transfers between devices, all_ahead(): moved.append(lax.ppermute(send, 'ctx', route))  10.2 us
    ppermute x1, starting transfers between devices, local(): lax.ppermute(rim, 'ctx', [(i, i + 1) for i in range(1, n_ctx - 1, 2)])  4.89 us
    ppermute x3, starting transfers between devices, local(): lax.ppermute(named, 'ctx', [(i, i - 2 * d) for i in range(2 * d, n_ctx)])  3.88 us
  transfers between devices with their start and end apart: 15, of which 4 were waited for; matrix products, arithmetic and copies ran while one was open for 1% of the time, Pallas kernels for 65%

profile of v3, /device:TPU:5, one launch (start us, length us, event | category | flops | bytes accessed | tf_op | source)
XLA Modules:
  0.0 172.3 jit_solution(15626037671767945776)
XLA Ops:
  0.0 0.9 pad_maximum_fusion.fold_in
  1.0 0.7 copy-done
  1.7 2.6 %prep.1 = (bf16[2640,128]{1,0:T(8,128)(2,1)S(1)}, bf16[1280,128]{1,0:T(8,128)(2,1)S(1)}, s32[1,32]{1,0:T(1,128)S(1)}, s32[4,32]{1,0:T(4,128)S(1)}, s32[4,32]{1,0...) custom-call(s32[7]{0:T(128)S(1)} %stack.31.where_ref.refs_0_, ...), custom_call_target="tpu_custom_call" | custom-call | tf_op jit(solution)/shard_map/prep/pallas_call | solution.py:673
  4.5 1.3 collective-permute-start.2
  5.8 1.3 collective-permute-start.1
  7.1 1.3 collective-permute-start
  8.4 1.0 copy.11
  9.4 1.1 pad.4.gate_ref.refs_4_
  10.6 0.4 collective-permute-done.1.refs_1_.refs_2_
  11.0 0.7 collective-permute-done.refs_0_.refs_1_
  11.6 0.6 pack.2
  12.3 4.9 %collective-permute-start.4 = (bf16[1280,128]{1,0:T(8,128)(2,1)S(1)}, bf16[1280,128]{1,0:T(8,128)(2,1)S(1)}, u32[]{:S(2)}, u32[]{:S(2)}) collective-permute-start(bf16[1280,128]{1,0:T(8,128)(2,1)S(1)} %get-tuple-element.59), channel_id=1, source_target_pairs={{4,8},{12,16},{20,24},{5,9},{13,17},{21,25},{6,10},{14,18},{22,26}... | collective-permute-start | bytes 983048 | tf_op jit(solution)/shard_map/ppermute | solution.py:727
  17.2 1.4 collective-permute-start.5
  18.6 3.4 %collective-permute-start.7 = (bf16[720,128]{1,0:T(8,128)(2,1)S(1)}, bf16[720,128]{1,0:T(8,128)(2,1)S(1)}, u32[]{:S(2)}, u32[]{:S(2)}) collective-permute-start(bf16[720,128]{1,0:T(8,128)(2,1)S(1)} %get-tuple-element.65), channel_id=1, source_target_pairs={{0,16},{4,20},{8,24},{12,28},{1,17},{5,21},{9,25},{13,29},{2,18},{... | collective-permute-start | bytes 552968 | tf_op jit(solution)/shard_map/ppermute | solution.py:720
  21.9 1.3 collective-permute-start.9
  23.2 25.6 %near_branch.2.refs_5_ = bf16[1024,2048]{1,0:T(8,128)(2,1)} custom-call(s32[7]{0:T(128)S(1)} %stack.31.where_ref.refs_0_, bf16[1024,3072]{1,0:T(8,128)(2,1)} %refs_3_.5, f32[1024,128]{1,0:T(8,128)S(1)} %pad.4.gate_ref.refs_4_, bf16[256,1024]{1,0:T(8,128)(2,1)S(1)} %get-tuple-element.55.refs_0_, bf16[256,1024]{1,0:T(8,128)(2,1)S(1)} %get-tuple-element.56.refs_1_, ...), custom_call_target="tpu_custom_call" | custom-call | flops 402653184 | bytes 7340032 | tf_op jit(solution)/shard_map/near_branch/pallas_call | solution.py:451
  48.8 0.6 pack.3
  49.4 1.3 collective-permute-start.6
  50.8 1.3 collective-permute-start.8
  52.1 1.5 collective-permute-start.10
  53.6 18.6 %near_branch.3.refs_5_ = bf16[1024,2048]{1,0:T(8,128)(2,1)} custom-call(s32[7]{0:T(128)S(1)} %stack.31.where_ref.refs_0_, bf16[1024,3072]{1,0:T(8,128)(2,1)} %refs_3_.5, f32[1024,128]{1,0:T(8,128)S(1)} %pad.4.gate_ref.refs_4_, bf16[256,1024]{1,0:T(8,128)(2,1)S(1)} %get-tuple-element.55.refs_0_, ...), custom_call_target="tpu_custom_call", output_to_operand_aliasing={{}: (8, {})} | custom-call | flops 402653184 | bytes 7340032 | tf_op jit(solution)/shard_map/near_branch/pallas_call | solution.py:451
  72.3 1.1 pool.1
  73.5 22.9 %chosen_and_project.4 = bf16[256,2560]{1,0:T(8,128)(2,1)S(1)} custom-call(s32[7]{0:T(128)S(1)} %stack.31.where_ref.refs_0_, s32[4,32]{1,0:T(4,128)S(1)} %get-tuple-element.42.refs_1_, s32[4,32]{1,0:T(4,128)S(1)} %get-tuple-element.43.refs_2_, bf16[1024,3072]{1,0:T(8,128)(2,1)} %refs_3_.5, f32[1024,128]{1,0:T(8,128)S(1)} %pad.4.gate_ref.refs_4_, ...), custom_call_target="tpu_custom_call" | custom-call | flops 268435456 | bytes 5242880 | tf_op jit(solution)/shard_map/chosen_and_project/pallas_call | solution.py:570
  96.4 2.4 %collective-permute-start.11 = (bf16[256,2560]{1,0:T(8,128)(2,1)S(1)}, bf16[256,2560]{1,0:T(8,128)(2,1)S(1)}, u32[]{:S(2)}, u32[]{:S(2)}) collective-permute-start(bf16[256,2560]{1,0:T(8,128)(2,1)S(1)} %chosen_and_project.4), channel_id=1, source_target_pairs={{0,1},{1,0},{2,3},{3,2},{4,5},{5,4},{6,7},{7,6},{8,9},{9,8},{10,11... | collective-permute-start | bytes 3932168 | tf_op jit(solution)/shard_map/ppermute | solution.py:765
  98.8 23.1 %chosen_and_project.3 = bf16[256,2560]{1,0:T(8,128)(2,1)S(1)} custom-call(s32[7]{0:T(128)S(1)} %stack.31.where_ref.refs_0_, s32[4,32]{1,0:T(4,128)S(1)} %get-tuple-element.42.refs_1_, s32[4,32]{1,0:T(4,128)S(1)} %get-tuple-element.43.refs_2_, bf16[1024,3072]{1,0:T(8,128)(2,1)} %refs_3_.5, f32[1024,128]{1,0:T(8,128)S(1)} %pad.4.gate_ref.refs_4_, ...), custom_call_target="tpu_custom_call" | custom-call | flops 268435456 | bytes 5242880 | tf_op jit(solution)/shard_map/chosen_and_project/pallas_call | solution.py:570
  122.0 0.3 add_convert_fusion
  122.3 1.3 collective-permute-start.14
  123.6 44.3 %chosen_and_project.5 = (bf16[256,1280]{1,0:T(8,128)(2,1)S(1)}, bf16[256,1280]{1,0:T(8,128)(2,1)S(1)}, bf16[256,2560]{1,0:T(8,128)(2,1)S(1)}) custom-call(s32[7]{0:T(128)S(1)} %stack.31.where_ref.refs_0_, s32[4,32]{1,0:T(4,128)S(1)} %get-tuple-element.42.refs_1_, s32[4,32]{1,0:T(4,128)S(1)} %get-tuple-element.43.refs_2_, bf16[1024,3072]{1,0:T(8,128)(2,1)} %refs_3_.5, ...), custom_call_target="tpu_custom_call" | custom-call | flops 268435456 | bytes 5242880 | tf_op jit(solution)/shard_map/chosen_and_project/pallas_call | solution.py:570
  167.8 0.4 collective-permute-start.12
  168.4 1.6 collective-permute-done.12.refs_0_
  170.0 0.9 collective-permute-done.13.refs_1_
  171.0 1.3 last_sum.1
  (18 shorter events, 0.5 us)
Async XLA Ops:
  1.0 0.7 copy-start
  1.7 6.6 %copy-start.1 = (f32[1024,3,16]{0,2,1:T(8,128)S(1)}, f32[1024,3,16]{0,2,1:T(8,128)}, u32[]{:S(2)}) copy-start(f32[1024,3,16]{0,2,1:T(8,128)} %param.14) | copy-start | bytes 589828
  4.4 44.4 %collective-permute-start.3 = (bf16[2640,128]{1,0:T(8,128)(2,1)S(1)}, bf16[2640,128]{1,0:T(8,128)(2,1)S(1)}, u32[]{:S(2)}, u32[]{:S(2)}) collective-permute-start(bf16[2640,128]{1,0:T(8,128)(2,1)S(1)} %get-tuple-element.49.refs_3_.own_ref), channel_id=1, source_target_pairs={{0,4},{4,0},{8,12},{12,8},{16,20},{20,16},{24,28},{28,24},{1,5},{5... | collective-permute-start | bytes 2027528 | tf_op jit(solution)/shard_map/ppermute | solution.py:695
  4.5 6.1 %collective-permute-start.2 = (s32[1,32]{1,0:T(1,128)S(1)}, s32[1,32]{1,0:T(1,128)S(1)}, u32[]{:S(2)}, u32[]{:S(2)}) collective-permute-start(s32[1,32]{1,0:T(1,128)S(1)} %get-tuple-element.61.refs_0_), channel_id=1, source_target_pairs={{24,0},{28,4},{25,1},{29,5},{26,2},{30,6},{27,3},{31,7}} | collective-permute-start | bytes 392 | tf_op jit(solution)/shard_map/ppermute | solution.py:697
  5.8 5.2 %collective-permute-start.1 = (s32[1,32]{1,0:T(1,128)S(1)}, s32[1,32]{1,0:T(1,128)S(1)}, u32[]{:S(2)}, u32[]{:S(2)}) collective-permute-start(s32[1,32]{1,0:T(1,128)S(1)} %get-tuple-element.61.refs_0_), channel_id=1, source_target_pairs={{16,0},{20,4},{24,8},{28,12},{17,1},{21,5},{25,9},{29,13},{18,2},{... | collective-permute-start | bytes 392 | tf_op jit(solution)/shard_map/ppermute | solution.py:697
  7.1 4.6 %collective-permute-start = (s32[1,32]{1,0:T(1,128)S(1)}, s32[1,32]{1,0:T(1,128)S(1)}, u32[]{:S(2)}, u32[]{:S(2)}) collective-permute-start(s32[1,32]{1,0:T(1,128)S(1)} %get-tuple-element.61.refs_0_), channel_id=1, source_target_pairs={{8,0},{12,4},{16,8},{20,12},{24,16},{28,20},{9,1},{13,5},{17,9},{2... | collective-permute-start | bytes 392 | tf_op jit(solution)/shard_map/ppermute | solution.py:697
  12.3 39.8 %collective-permute-start.4 = (bf16[1280,128]{1,0:T(8,128)(2,1)S(1)}, bf16[1280,128]{1,0:T(8,128)(2,1)S(1)}, u32[]{:S(2)}, u32[]{:S(2)}) collective-permute-start(bf16[1280,128]{1,0:T(8,128)(2,1)S(1)} %get-tuple-element.59), channel_id=1, source_target_pairs={{4,8},{12,16},{20,24},{5,9},{13,17},{21,25},{6,10},{14,18},{22,26}... | collective-permute-start | bytes 983048 | tf_op jit(solution)/shard_map/ppermute | solution.py:727
  17.2 33.6 %collective-permute-start.5 = (bf16[720,128]{1,0:T(8,128)(2,1)S(1)}, bf16[720,128]{1,0:T(8,128)(2,1)S(1)}, u32[]{:S(2)}, u32[]{:S(2)}) collective-permute-start(bf16[720,128]{1,0:T(8,128)(2,1)S(1)} %get-tuple-element.63), channel_id=1, source_target_pairs={{0,24},{4,28},{1,25},{5,29},{2,26},{6,30},{3,27},{7,31}} | collective-permute-start | bytes 552968 | tf_op jit(solution)/shard_map/ppermute | solution.py:720
  18.6 53.7 %collective-permute-start.7 = (bf16[720,128]{1,0:T(8,128)(2,1)S(1)}, bf16[720,128]{1,0:T(8,128)(2,1)S(1)}, u32[]{:S(2)}, u32[]{:S(2)}) collective-permute-start(bf16[720,128]{1,0:T(8,128)(2,1)S(1)} %get-tuple-element.65), channel_id=1, source_target_pairs={{0,16},{4,20},{8,24},{12,28},{1,17},{5,21},{9,25},{13,29},{2,18},{... | collective-permute-start | bytes 552968 | tf_op jit(solution)/shard_map/ppermute | solution.py:720
  21.9 50.4 %collective-permute-start.9 = (bf16[720,128]{1,0:T(8,128)(2,1)S(1)}, bf16[720,128]{1,0:T(8,128)(2,1)S(1)}, u32[]{:S(2)}, u32[]{:S(2)}) collective-permute-start(bf16[720,128]{1,0:T(8,128)(2,1)S(1)} %get-tuple-element.67), channel_id=1, source_target_pairs={{0,8},{4,12},{8,16},{12,20},{16,24},{20,28},{1,9},{5,13},{9,17},{1... | collective-permute-start | bytes 552968 | tf_op jit(solution)/shard_map/ppermute | solution.py:720
  49.4 22.8 %collective-permute-start.6 = (bf16[720,128]{1,0:T(8,128)(2,1)S(1)}, bf16[720,128]{1,0:T(8,128)(2,1)S(1)}, u32[]{:S(2)}, u32[]{:S(2)}) collective-permute-start(bf16[720,128]{1,0:T(8,128)(2,1)S(1)} %get-tuple-element.64), channel_id=1, source_target_pairs={{0,24},{4,28},{1,25},{5,29},{2,26},{6,30},{3,27},{7,31}} | collective-permute-start | bytes 552968 | tf_op jit(solution)/shard_map/ppermute | solution.py:720
  50.8 21.5 %collective-permute-start.8 = (bf16[720,128]{1,0:T(8,128)(2,1)S(1)}, bf16[720,128]{1,0:T(8,128)(2,1)S(1)}, u32[]{:S(2)}, u32[]{:S(2)}) collective-permute-start(bf16[720,128]{1,0:T(8,128)(2,1)S(1)} %get-tuple-element.66), channel_id=1, source_target_pairs={{0,16},{4,20},{8,24},{12,28},{1,17},{5,21},{9,25},{13,29},{2,18},{... | collective-permute-start | bytes 552968 | tf_op jit(solution)/shard_map/ppermute | solution.py:720
  52.1 20.2 %collective-permute-start.10 = (bf16[720,128]{1,0:T(8,128)(2,1)S(1)}, bf16[720,128]{1,0:T(8,128)(2,1)S(1)}, u32[]{:S(2)}, u32[]{:S(2)}) collective-permute-start(bf16[720,128]{1,0:T(8,128)(2,1)S(1)} %get-tuple-element.68), channel_id=1, source_target_pairs={{0,8},{4,12},{8,16},{12,20},{16,24},{20,28},{1,9},{5,13},{9,17},{1... | collective-permute-start | bytes 552968 | tf_op jit(solution)/shard_map/ppermute | solution.py:720
  96.4 25.6 %collective-permute-start.11 = (bf16[256,2560]{1,0:T(8,128)(2,1)S(1)}, bf16[256,2560]{1,0:T(8,128)(2,1)S(1)}, u32[]{:S(2)}, u32[]{:S(2)}) collective-permute-start(bf16[256,2560]{1,0:T(8,128)(2,1)S(1)} %chosen_and_project.4), channel_id=1, source_target_pairs={{0,1},{1,0},{2,3},{3,2},{4,5},{5,4},{6,7},{7,6},{8,9},{9,8},{10,11... | collective-permute-start | bytes 3932168 | tf_op jit(solution)/shard_map/ppermute | solution.py:765
  122.3 48.7 %collective-permute-start.14 = (bf16[256,2560]{1,0:T(8,128)(2,1)S(1)}, bf16[256,2560]{1,0:T(8,128)(2,1)S(1)}, u32[]{:S(2)}, u32[]{:S(2)}) collective-permute-start(bf16[256,2560]{1,0:T(8,128)(2,1)S(1)} %add_convert_fusion), channel_id=1, source_target_pairs={{0,2},{1,3},{2,0},{3,1},{4,6},{5,7},{6,4},{7,5},{8,10},{9,11},{10,... | collective-permute-start | bytes 3932168 | tf_op jit(solution)/shard_map/ppermute | solution.py:775
  167.8 2.2 %collective-permute-start.12 = (bf16[256,1280]{1,0:T(8,128)(2,1)S(1)}, bf16[256,1280]{1,0:T(8,128)(2,1)S(1)}, u32[]{:S(2)}, u32[]{:S(2)}) collective-permute-start(bf16[256,1280]{1,0:T(8,128)(2,1)S(1)} %get-tuple-element.76), channel_id=1, source_target_pairs={{0,1},{1,0},{2,3},{3,2},{4,5},{5,4},{6,7},{7,6},{8,9},{9,8},{10,11... | collective-permute-start | bytes 1966088 | tf_op jit(solution)/shard_map/ppermute | solution.py:771
  168.2 2.7 %collective-permute-start.13 = (bf16[256,1280]{1,0:T(8,128)(2,1)S(1)}, bf16[256,1280]{1,0:T(8,128)(2,1)S(1)}, u32[]{:S(2)}, u32[]{:S(2)}) collective-permute-start(bf16[256,1280]{1,0:T(8,128)(2,1)S(1)} %get-tuple-element.77), channel_id=1, source_target_pairs={{0,1},{1,0},{2,3},{3,2},{4,5},{5,4},{6,7},{7,6},{8,9},{9,8},{10,11... | collective-permute-start | bytes 1966088 | tf_op jit(solution)/shard_map/ppermute | solution.py:771
